TPU v7x, 256 devices: a whole 4x4x8 slice. The times are simulated.
256 devices in a mesh: gy: 16 (over y, z_lo), gz: 16 (over z_hi, x, core).
Axes of the slice: x: 4, y: 4, z: 8 (z_hi: 2, z_lo: 4; z = z_hi * 4 + z_lo), core: 2. Of those that a mesh axis runs over, the one named last changes fastest.
Arguments:
- velocity: float32 [3, 128, 32, 256], P(None, 'gy', 'gz'), may hold values from -6 to 6
- hidden: bfloat16 [32, 128, 32, 256], P(None, 'gy', 'gz'), may hold values from -3 to 3
- cell: float32 [32, 128, 32, 256], P(None, 'gy', 'gz'), may hold values from -6 to 6
- gate_weight: bfloat16 [128, 945], replicated, may hold values from -0.1875 to 0.1875
- gate_bias: float32 [128], replicated, may hold values from -1 to 1
- decoder: bfloat16 [3, 32], replicated, may hold values from -1 to 1
Outputs:
- hidden_next: bfloat16 [32, 128, 32, 256], P(None, 'gy', 'gz')
- cell_next: float32 [32, 128, 32, 256], P(None, 'gy', 'gz')
- velocity_next: float32 [3, 128, 32, 256], P(None, 'gy', 'gz')
All inputs are finite; a program needn't handle non-finite values.
Results may differ from a plain program's by a relative error of at most 0.0025.
Values may be sent and summed in bfloat16 or wider, within the bound.
A program may use at most 64 MiB of HBM per device.

v0:
```python
import functools

import jax
import jax.numpy as jnp
import numpy as np
from jax import lax
from jax.experimental import pallas as pl
from jax.experimental.pallas import tpu as pltpu
from jax.sharding import PartitionSpec as P

F32 = jnp.float32
BF16 = jnp.bfloat16
MESH = pl.DeviceIdType.MESH
NX, NY, NZ = 256, 128, 32
RANKS = 16
SLAB = 128
HALO = [(sy, sz) for sz in (-1, 1) for sy in (0, -1, 1)] + [(-1, 0), (1, 0)]


def halves(table):
    high = table.astype(np.float32).astype(jnp.bfloat16)
    low = (table - high.astype(np.float64)).astype(np.float32).astype(jnp.bfloat16)
    return np.stack([np.asarray(high), np.asarray(low)])


def signed_waves(total):
    index = np.arange(total)
    wave = np.where(index < total // 2, index, index - total)
    return np.where(index == total // 2, 0, wave).astype(np.float64)


def x_tables():
    lane = np.arange(128)
    mode = (lane % 16) * 8 + lane // 16
    n = np.arange(NX)
    angle = 2 * np.pi / NX * ((n[:, None] * mode[None, :]) % NX)
    sign = np.where(n % 2 == 0, 1.0, -1.0)
    imag = np.where(mode[None, :] == 0, sign[:, None], -np.sin(angle))
    forward = np.concatenate([np.cos(angle), imag], 1)
    weight = np.where(mode == 0, 1.0, 2.0)
    inverse = forward.T * np.concatenate([weight, weight])[:, None]
    return forward, inverse


def y_tables():
    lane = np.arange(128)
    mode = (lane % 16) * 8 + lane // 16
    y = np.arange(NY)
    angle = 2 * np.pi / NY * ((y[:, None] * mode[None, :]) % NY)
    forward = np.concatenate([np.cos(angle), np.sin(angle)], 0)
    inverse = np.concatenate([np.cos(angle).T, np.sin(angle).T], 0)
    return forward, inverse


def z_tables():
    kz = np.arange(NZ)
    z = np.arange(NZ)
    wave = signed_waves(NZ)[:, None]
    angle = 2 * np.pi / NZ * ((kz[:, None] * z[None, :]) % NZ)
    cosine, sine = np.cos(angle), np.sin(angle)
    forward = np.zeros((2, NZ, RANKS, 2, 2, 2))
    inverse = np.zeros((RANKS, 2, 2, 2, 2, NZ))
    for own in range(2):
        c, s = cosine[:, own::2], sine[:, own::2]
        for field, scale in ((0, np.ones_like(wave)), (1, wave)):
            forward[0, :, :, field, own, 0] = scale * c
            forward[0, :, :, field, own, 1] = scale * s
            forward[1, :, :, field, own, 1] = scale * c
            forward[1, :, :, field, own, 0] = -scale * s
            inverse[:, field, own, 0, 0, :] = (scale * c).T
            inverse[:, field, own, 0, 1, :] = -(scale * s).T
            inverse[:, field, own, 1, 1, :] = (scale * c).T
            inverse[:, field, own, 1, 0, :] = (scale * s).T
    return forward.reshape(64, 128), inverse.reshape(128, 64)


def split(value):
    high = value.astype(BF16)
    return high, (value - high.astype(F32)).astype(BF16)


def dot(a, b):
    return jnp.dot(a, b, preferred_element_type=F32)


def data_by_table(value, table):
    high, low = split(value)
    return dot(high, table[0]) + (dot(low, table[0]) + dot(high, table[1]))


def table_by_data(table, value):
    high, low = split(value)
    return dot(table[0], high) + (dot(table[0], low) + dot(table[1], high))


def roll_lanes(value, shift):
    return value if shift % 128 == 0 else pltpu.roll(value, shift % 128, 1)


def roll_rows(value, shift):
    return pltpu.roll(value, shift % value.shape[0], 0)


def lane_ids():
    return lax.broadcasted_iota(jnp.int32, (8, 128), 1)


def lane_mix(values, count):
    low = lane_ids() % 16
    masks = [low == q for q in range(16)]
    rolled = [roll_lanes(v, r) for r, v in enumerate(values)]
    outs = []
    for j in range(count):
        acc = jnp.zeros((8, 128), F32)
        for r, v in enumerate(rolled):
            acc = jnp.where(masks[(j + r) % 16], v, acc)
        outs.append(roll_lanes(acc, -j))
    return outs


def wave_of(index, total):
    wave = jnp.where(index < total // 2, index, index - total)
    return jnp.where(index == total // 2, 0, wave).astype(F32)


def mode_waves(total):
    lane = lane_ids()
    return wave_of((lane % 16) * 8 + lane // 16, total)


def x_forward(rows, table):
    spectrum = data_by_table(rows, table)
    kx = mode_waves(2 * NX)

    def part(c, z, p):
        start = (2 * c + z) * 8
        return spectrum[start : start + 8, 128 * p : 128 * p + 128]

    values = []
    for c in (0, 2, 1):
        for z in range(2):
            for p in range(2):
                values.append(part(c, z, p) * kx if c == 0 else part(c, z, p))
    return lane_mix(values, RANKS)


def swapped(value, sign):
    even = lax.broadcasted_iota(jnp.int32, value.shape, 0) % 2 == 0
    return jnp.where(even, sign * roll_rows(value, -1), -sign * roll_rows(value, 1))


def y_forward(tiles, table):
    rows = tiles.T
    out = data_by_table(jnp.concatenate([rows, swapped(rows, 1.0)], 1), table)
    ky = mode_waves(NY)
    values = [out[16 * k : 16 * k + 8] + ky * out[16 * k + 8 : 16 * k + 16] for k in range(8)]
    return lane_mix(values, RANKS)


def z_both(tiles, forward, inverse, me_gy, me_gz):
    numer = table_by_data(forward, tiles)
    lane = lax.broadcasted_iota(jnp.int32, (NZ, 128), 1)
    kx = (me_gy * 8 + lane % 8).astype(F32)
    ky = wave_of(me_gz * 8 + lane // 16, NY)
    kz = wave_of(lax.broadcasted_iota(jnp.int32, (NZ, 128), 0), NZ)
    factor = (1.0 / (NX * NY * NZ)) / jnp.maximum(kx * kx + ky * ky + kz * kz, 1.0)
    return table_by_data(inverse, numer * jnp.concatenate([factor, factor], 0))


def y_inverse(tiles, table):
    values = lane_mix(tiles, 8)
    ky = mode_waves(NY)
    rows = []
    for v in values:
        rows += [v, v * ky]
    rows = jnp.concatenate(rows, 0)
    out = data_by_table(jnp.concatenate([rows, swapped(rows, -1.0)], 1), table)
    return out.T


def x_inverse(tiles, table):
    values = lane_mix(tiles, 12)
    kx = mode_waves(2 * NX)
    rows = []
    for c, base in ((0, 0), (1, 8), (2, 4)):
        for z in range(2):
            pair = [values[base + 2 * z + p] for p in range(2)]
            if c == 0:
                pair = [v * kx for v in pair]
            rows.append(jnp.concatenate(pair, 1))
    return data_by_table(jnp.concatenate(rows, 0), table)


def around(index, step):
    return lax.rem(index + step + RANKS, RANKS)


def spectral_kernel(
    u_ref, xf_ref, xi_ref, yf_ref, yi_ref, zf_ref, zi_ref, out_ref, send, recv, send_sem, recv_sem
):
    gy, gz = lax.axis_index("gy"), lax.axis_index("gz")
    barrier = pltpu.get_barrier_semaphore()

    def greet(d, carry):
        pl.semaphore_signal(barrier, inc=1, device_id=(around(gy, d), gz), device_id_type=MESH)
        pl.semaphore_signal(barrier, inc=1, device_id=(gy, around(gz, d)), device_id_type=MESH)
        return carry

    lax.fori_loop(1, RANKS, greet, 0)

    def exchange(step, along_y):
        me = gy if along_y else gz

        def start(d, carry):
            to = around(me, d)
            target = (to, gz) if along_y else (gy, to)
            pltpu.make_async_remote_copy(
                src_ref=send.at[step, to],
                dst_ref=recv.at[step, me],
                send_sem=send_sem.at[step],
                recv_sem=recv_sem.at[step],
                device_id=target,
                device_id_type=MESH,
            ).start()
            return carry

        lax.fori_loop(1, RANKS, start, 0)
        recv[step, pl.ds(me, 1)] = send[step, pl.ds(me, 1)]
        some = recv.at[step, pl.ds(0, RANKS - 1)]
        pltpu.make_async_copy(some, some, recv_sem.at[step]).wait()

    tiles = x_forward(u_ref[...], xf_ref)
    for j in range(RANKS):
        send[0, j] = tiles[j]
    pl.semaphore_wait(barrier, 2 * (RANKS - 1))
    exchange(0, True)
    tiles = y_forward(recv[0].reshape(128, 128), yf_ref)
    for j in range(RANKS):
        send[1, j] = tiles[j]
    exchange(1, False)
    send[2] = z_both(recv[1].reshape(128, 128), zf_ref, zi_ref, gy, gz).reshape(RANKS, 8, 128)
    exchange(2, False)
    send[3] = y_inverse([recv[2, j] for j in range(RANKS)], yi_ref).reshape(RANKS, 8, 128)
    exchange(3, True)
    gradient = x_inverse([recv[3, j] for j in range(RANKS)], xi_ref)
    result = u_ref[...] - gradient
    for c in range(3):
        for z in range(2):
            start = (2 * c + z) * 8
            for t in range(2):
                out_ref[pl.ds(c * 32 + 2 * t + z, 8, stride=4), :] = result[
                    start : start + 8, 128 * t : 128 * t + 128
                ]
    for step in range(4):
        some = send.at[step, pl.ds(0, RANKS - 1)]
        pltpu.make_async_copy(some, some, send_sem.at[step]).wait()


def conv_kernel(
    vel_hbm, hid_hbm, cell_hbm, weight_hbm, bias_ref, dec_ref, hid_out, cell_out, u_ref,
    hid_in, hid_f, vel_f, cell_v, weight_v, weight_f, block_f, wide, side, slabs, vels, vel_t,
    vz_s, vz_r, vy_s, vy_r, vc_s, vc_r, acc, moved, load_sem, send_sem, recv_sem, store_sem,
):
    gy, gz = lax.axis_index("gy"), lax.axis_index("gz")
    loads = [
        pltpu.make_async_copy(src, dst, load_sem.at[i])
        for i, (src, dst) in enumerate(
            [(hid_hbm, hid_in), (vel_hbm, vel_f), (weight_hbm, weight_v), (cell_hbm, cell_v)]
        )
    ]
    for load in loads:
        load.start()
    barrier = pltpu.get_barrier_semaphore()
    targets = [(around(gy, sy), around(gz, sz)) for sy, sz in HALO]
    for target in targets:
        pl.semaphore_signal(barrier, inc=1, device_id=target, device_id_type=MESH)
    vels[...] = jnp.zeros_like(vels)

    loads[0].wait()
    hid_f[...] = hid_in[...].astype(F32)
    loads[1].wait()

    def centre(y, carry):
        for z in range(2):
            for t in range(2):
                lanes = slice(128 * t, 128 * t + 128)
                rows = hid_f[pl.ds(y * 4 + 2 * t + z, 32, stride=32), :]
                slabs[y + 1, z + 1, 32:64, lanes] = rows.astype(BF16)
                vels[y + 1, z + 1, 0:3, lanes] = vel_f[pl.ds(y * 4 + 2 * t + z, 3, stride=32), :]
        return carry

    lax.fori_loop(0, 8, centre, 0)
    for z in range(2):
        for t in range(2):
            rows = vel_f[pl.ds(2 * t + z, 24, stride=4), :]
            rows = jnp.concatenate([rows, jnp.zeros((8, 128), F32)], 0)
            vz_s[z, :, 128 * t : 128 * t + 128] = rows.astype(BF16)
    for k in range(2):
        y = 1 + 7 * k
        vy_s[k] = jnp.concatenate([vels[y, 1], vels[y, 2]], 0).astype(BF16)
        for z in range(2):
            rows = jnp.concatenate([vels[y, z + 1], jnp.zeros((8, NX), F32)], 0)
            vc_s[2 * k + z] = rows.astype(BF16)

    pl.semaphore_wait(barrier, len(HALO))
    copies = []
    for i, (sy, sz) in enumerate(HALO):
        k, z = (1 + sy) // 2, (1 + sz) // 2
        src_y, dst_y = (pl.ds(1, 8), pl.ds(1, 8)) if sy == 0 else (pl.ds(1 + 7 * k, 1), pl.ds(9 - 9 * k, 1))
        src_z, dst_z = (pl.ds(1, 2), pl.ds(1, 2)) if sz == 0 else (pl.ds(1 + z, 1), pl.ds(3 - 3 * z, 1))
        if sy == 0:
            extra = (vz_s.at[z], vz_r.at[z])
        elif sz == 0:
            extra = (vy_s.at[k], vy_r.at[k])
        else:
            extra = (vc_s.at[2 * k + z], vc_r.at[2 * k + z])
        mids = pl.ds(32, 32)
        pair = []
        for n, (src, dst) in enumerate(
            [(slabs.at[src_y, src_z, mids], slabs.at[dst_y, dst_z, mids]), extra]
        ):
            pair.append(
                pltpu.make_async_remote_copy(
                    src_ref=src,
                    dst_ref=dst,
                    send_sem=send_sem.at[i, n],
                    recv_sem=recv_sem.at[i, n],
                    device_id=targets[i],
                    device_id_type=MESH,
                )
            )
            pair[-1].start()
        copies.append(pair)

    def fill(y, z):
        mid = slabs[y, z, 32:64, :].astype(F32)
        slabs[y, z, 0:32, :] = pltpu.roll(mid, 1, 1).astype(BF16)
        slabs[y, z, 64:96, :] = pltpu.roll(mid, NX - 1, 1).astype(BF16)
        v = vels[y, z]
        first = v + pltpu.roll(pltpu.roll(v, 1, 1), 3, 0)
        tile = jnp.concatenate([first, pltpu.roll(v, NX - 1, 1), jnp.ones((16, NX), F32)], 0)
        slabs[y, z, 96:128, :] = tile.astype(BF16)

    def fill_own(y, carry):
        fill(y, 1)
        fill(y, 2)
        return carry

    lax.fori_loop(1, 9, fill_own, 0)

    loads[2].wait()
    weight_f[0:945, :] = weight_v[...].astype(F32)
    block_f[96:128, :] = jnp.zeros((32, 128), F32)
    for dy in range(3):
        for dz in range(3):
            first = (9 * dy + 3 * dz) * 35
            for dx in range(3):
                at = first + 35 * dx
                block_f[32 * dx : 32 * dx + 32, :] = weight_f[at + 3 : at + 35, :]
                row = 96 + (3, 0, 8)[dx]
                block_f[row : row + 3, :] = weight_f[at : at + 3, :]
            if dy == 1 and dz == 1:
                rest = bias_ref[...]
                for part in range(3):
                    high = rest.astype(BF16).astype(F32)
                    block_f[112 + part : 113 + part, :] = high
                    rest = rest - high
            turned = block_f[...].T.astype(BF16)
            if dy == 1 and dz == 1:
                block_f[112:120, :] = jnp.zeros((8, 128), F32)
            if dz == 0:
                side[0, :, 128 * dy : 128 * dy + 128] = turned
            if dz == 2:
                side[1, :, 128 * dy : 128 * dy + 128] = turned
            for z in range(2):
                own = z + dz - 1
                if 0 <= own < 2:
                    at = (2 * dy + own) * 128
                    wide[128 * z : 128 * z + 128, at : at + 128] = turned

    def inner(y):
        acc[y] = dot(wide[...], slabs[pl.ds(y, 3), 1:3].reshape(6 * SLAB, NX))

    def inner_step(y, carry):
        inner(y)
        return carry

    lax.fori_loop(1, 7, inner_step, 0)

    for i in (6, 7):
        for copy in copies[i]:
            copy.wait_recv()
        k = (1 + HALO[i][0]) // 2
        rows = vy_r[k].astype(F32)
        y = 9 - 9 * k
        vels[y, 1] = rows[0:8]
        vels[y, 2] = rows[8:16]
        fill(y, 1)
        fill(y, 2)
    inner(0)
    inner(7)

    for i in range(6):
        for copy in copies[i]:
            copy.wait_recv()
    for z in range(2):
        to = 3 - 3 * z
        rows = vz_r[z].astype(F32)
        for t in range(2):
            vel_t[t] = rows[:, 128 * t : 128 * t + 128]
            for y in range(8):
                vels[y + 1, to, 0:3, 128 * t : 128 * t + 128] = vel_t[t, pl.ds(y, 3, stride=8), :]
        for k in range(2):
            vels[9 - 9 * k, to] = vc_r[2 * k + z].astype(F32)[0:8]

    def fill_outer(y, carry):
        fill(y, 0)
        fill(y, 3)
        return carry

    lax.fori_loop(0, 10, fill_outer, 0)

    loads[3].wait()

    def sigmoid(value):
        return 0.5 * jnp.tanh(0.5 * value) + 0.5

    def update(y, carry):
        for z in range(2):
            outer = slabs[pl.ds(y, 3), 3 * z].reshape(3 * SLAB, NX)
            gates = acc[y, 128 * z : 128 * z + 128, :] + dot(side[z], outer)
            hidden_parts = []
            for t in range(2):
                lanes = slice(128 * t, 128 * t + 128)
                rows = pl.ds(y * 4 + 2 * t + z, 32, stride=32)
                part = gates[:, lanes]
                cell = sigmoid(part[32:64]) * cell_v[rows, :] + sigmoid(part[0:32]) * jnp.tanh(part[64:96])
                hidden = sigmoid(part[96:128]) * jnp.tanh(cell)
                cell_v[rows, :] = cell
                hid_f[rows, :] = hidden
                hidden_parts.append(hidden.astype(BF16))
            increment = dot(dec_ref[...], jnp.concatenate(hidden_parts, 1))
            advanced = vels[y + 1, z + 1, 0:3, :] + increment
            for t in range(2):
                rows = pl.ds(pl.multiple_of(16 * y + 8 * z, 8), 3)
                moved[t, rows, :] = advanced[:, 128 * t : 128 * t + 128]
        return carry

    lax.fori_loop(0, 8, update, 0)
    for c in range(3):
        for z in range(2):
            for t in range(2):
                start = 16 * c + 8 * z
                u_ref[start : start + 8, 128 * t : 128 * t + 128] = moved[
                    t, pl.ds(8 * z + c, 8, stride=16), :
                ]
    cell_store = pltpu.make_async_copy(cell_v, cell_out, store_sem.at[0])
    cell_store.start()
    hid_in[...] = hid_f[...].astype(BF16)
    hid_store = pltpu.make_async_copy(hid_in, hid_out, store_sem.at[1])
    hid_store.start()
    for pair in copies:
        for copy in pair:
            copy.wait_send()
    cell_store.wait()
    hid_store.wait()


def to_rows(array):
    c = array.shape[0]
    return array.reshape(c, 8, 2, 2, 128).transpose(0, 1, 3, 2, 4).reshape(c * 32, 128)


def from_rows(array):
    c = array.shape[0] // 32
    return array.reshape(c, 8, 2, 2, 128).transpose(0, 1, 3, 2, 4).reshape(c, 8, 2, 256)


def per_device(velocity, hidden, cell, gate_weight, gate_bias, decoder):
    vmem = pl.BlockSpec(memory_space=pltpu.VMEM)
    anywhere = pl.BlockSpec(memory_space=pl.ANY)
    hid_next, cell_next, advanced = pl.pallas_call(
        conv_kernel,
        out_shape=(
            jax.ShapeDtypeStruct((1024, 128), BF16),
            jax.ShapeDtypeStruct((1024, 128), F32),
            jax.ShapeDtypeStruct((48, 256), F32),
        ),
        in_specs=[anywhere] * 4 + [vmem] * 2,
        out_specs=(anywhere, anywhere, vmem),
        scratch_shapes=[
            pltpu.VMEM((1024, 128), BF16),
            pltpu.VMEM((1024, 128), F32),
            pltpu.VMEM((96, 128), F32),
            pltpu.VMEM((1024, 128), F32),
            pltpu.VMEM((945, 128), BF16),
            pltpu.VMEM((952, 128), F32),
            pltpu.VMEM((128, 128), F32),
            pltpu.VMEM((256, 768), BF16),
            pltpu.VMEM((2, 128, 384), BF16),
            pltpu.VMEM((10, 4, SLAB, NX), BF16),
            pltpu.VMEM((10, 4, 8, NX), F32),
            pltpu.VMEM((2, 32, 128), F32),
            pltpu.VMEM((2, 32, NX), BF16),
            pltpu.VMEM((2, 32, NX), BF16),
            pltpu.VMEM((2, 16, NX), BF16),
            pltpu.VMEM((2, 16, NX), BF16),
            pltpu.VMEM((4, 16, NX), BF16),
            pltpu.VMEM((4, 16, NX), BF16),
            pltpu.VMEM((8, 256, 256), F32),
            pltpu.VMEM((2, 128, 128), F32),
            pltpu.SemaphoreType.DMA((4,)),
            pltpu.SemaphoreType.DMA((8, 2)),
            pltpu.SemaphoreType.DMA((8, 2)),
            pltpu.SemaphoreType.DMA((2,)),
        ],
        compiler_params=pltpu.CompilerParams(
            collective_id=0, has_side_effects=True, vmem_limit_bytes=24 * 1024 * 1024
        ),
    )(
        to_rows(velocity),
        to_rows(hidden),
        to_rows(cell),
        gate_weight.T,
        gate_bias.reshape(1, 128),
        decoder,
    )
    tables = [jnp.asarray(halves(t)) for t in (*x_tables(), *y_tables(), *z_tables())]
    velocity_next = pl.pallas_call(
        spectral_kernel,
        out_shape=jax.ShapeDtypeStruct((96, 128), F32),
        in_specs=[vmem] * 7,
        out_specs=vmem,
        scratch_shapes=[
            pltpu.VMEM((4, RANKS, 8, 128), F32),
            pltpu.VMEM((4, RANKS, 8, 128), F32),
            pltpu.SemaphoreType.DMA((4,)),
            pltpu.SemaphoreType.DMA((4,)),
        ],
        compiler_params=pltpu.CompilerParams(
            collective_id=1, has_side_effects=True, vmem_limit_bytes=16 * 1024 * 1024
        ),
    )(advanced, *tables)
    return from_rows(hid_next), from_rows(cell_next), from_rows(velocity_next)


def solution(mesh):
    field = P(None, "gy", "gz", None)
    return jax.shard_map(
        per_device,
        mesh=mesh,
        in_specs=(field, field, field, P(), P(), P()),
        out_specs=(field, field, field),
        check_vma=False,
    )
```

profile of v0, /device:TPU:1, one launch (start us, length us, event | category | flops | bytes accessed | tf_op | source)
XLA Modules:
  0.0 61.9 jit_solution(18129136020827061771)
XLA Ops:
  0.6 0.0 copy-start.10
  0.6 0.0 copy-start.11
  0.7 0.7 %copy-done.10 = bf16[3,32]{1,0:T(4,128)(2,1)S(1)} copy-done((bf16[3,32]{1,0:T(4,128)(2,1)S(1)}, bf16[3,32]{1,0:T(4,128)(2,1)}, u32[]{:S(2)}) %copy-start.10) | copy-done | bytes 216
  1.3 0.0 copy-done.11
  1.3 0.0 copy-start
  1.3 1.0 %copy-done = f32[32,8,2,256]{3,2,1,0:T(2,128)S(1)} copy-done((f32[32,8,2,256]{3,2,1,0:T(2,128)S(1)}, f32[32,8,2,256]{3,2,1,0:T(2,128)}, u32[]{:S(2)}) %copy-start) | copy-done | bytes 524312
  2.4 0.0 copy-start.1
  2.4 0.9 %copy-done.1 = bf16[32,8,2,256]{3,2,1,0:T(2,128)(2,1)S(1)} copy-done((bf16[32,8,2,256]{3,2,1,0:T(2,128)(2,1)S(1)}, bf16[32,8,2,256]{3,2,1,0:T(2,128)(2,1)}, u32[]{:S(2)}) %copy-start.1) | copy-done | bytes 262168
  3.3 0.0 copy-start.4
  3.3 0.9 %copy-done.4 = bf16[128,945]{0,1:T(8,128)(2,1)S(1)} copy-done((bf16[128,945]{0,1:T(8,128)(2,1)S(1)}, bf16[128,945]{0,1:T(8,128)(2,1)}, u32[]{:S(2)}) %copy-start.4) | copy-done | bytes 241944
  4.3 0.0 copy-start.8
  4.3 0.8 %copy-done.8 = f32[3,8,2,256]{3,2,1,0:T(2,128)S(1)} copy-done((f32[3,8,2,256]{3,2,1,0:T(2,128)S(1)}, f32[3,8,2,256]{3,2,1,0:T(2,128)}, u32[]{:S(2)}) %copy-start.8) | copy-done | bytes 49176
  5.1 0.0 copy-start.2
  5.1 0.0 copy-start.3
  5.1 0.0 copy-start.5
  5.1 0.0 copy-start.6
  5.1 0.0 copy-start.7
  5.1 0.0 copy-start.9
  5.1 25.5 %shard_map.139 = (bf16[1024,128]{1,0:T(8,128)(2,1)S(1)}, f32[1024,128]{1,0:T(8,128)S(1)}, f32[48,256]{1,0:T(8,128)S(1)}) custom-call(f32[96,128]{1,0:T(8,128)S(1)} %bitcast.38, bf16[1024,128]{1,0:T(8,128)(2,1)S(1)} %bitcast.34, f32[1024,128]{1,0:T(8,128)S(1)} %bitcast.32, bf16[945,128]{1,0:T(8,128)(2,1)S(1)} %bitcast.36, f32[1,128]{1,0:T(1,128)S(1)} %bitcast.39, ...), custom_call_target="tpu_custom_call" | custom-call | tf_op jit(solution)/shard_map/pallas_call | solution.py:482
  30.6 0.0 copy-done.2
  30.6 0.0 copy-done.3
  30.6 0.0 copy-done.5
  30.6 0.0 copy-done.6
  30.6 0.0 copy-done.7
  30.6 0.0 copy-done.9
  30.6 29.1 %shard_map.140 = f32[96,128]{1,0:T(8,128)S(1)} custom-call(f32[48,256]{1,0:T(8,128)S(1)} %get-tuple-element.8.u_ref, bf16[2,256,256]{2,1,0:T(8,128)(2,1)S(1)} %copy-done.3, bf16[2,256,256]{2,1,0:T(8,128)(2,1)S(1)} %copy-done.2, bf16[2,256,128]{2,1,0:T(8,128)(2,1)S(1)} %copy-done.6, bf16[2,256,128]{2,1,0:T(8,128)(2,1)S(1)} %copy-done.5, ...), custom_call_target="tpu_custom_call" | custom-call | tf_op jit(solution)/shard_map/pallas_call | solution.py:529
  59.7 0.7 %copy.24 = bf16[32,8,2,256]{3,2,1,0:T(2,128)(2,1)} copy(bf16[32,8,2,256]{3,2,1,0:T(2,128)(2,1)S(1)} %bitcast.35) | data formatting | bytes 524288
  60.4 0.8 %copy.25 = f32[32,8,2,256]{3,2,1,0:T(2,128)} copy(f32[32,8,2,256]{3,2,1,0:T(2,128)S(1)} %bitcast.33) | data formatting | bytes 1048576
  61.2 0.6 %copy.26 = f32[3,8,2,256]{3,2,1,0:T(2,128)} copy(f32[3,8,2,256]{3,2,1,0:T(2,128)S(1)} %bitcast.37) | data formatting | bytes 98304
Async XLA Ops:
  0.6 0.7 %copy-start.10 = (bf16[3,32]{1,0:T(4,128)(2,1)S(1)}, bf16[3,32]{1,0:T(4,128)(2,1)}, u32[]{:S(2)}) copy-start(bf16[3,32]{1,0:T(4,128)(2,1)} %dec_ref.1) | copy-start | bytes 580
  0.6 0.7 %copy-start.11 = (f32[128]{0:T(128)S(1)}, f32[128]{0:T(128)}, u32[]{:S(2)}) copy-start(f32[128]{0:T(128)} %param.16) | copy-start | bytes 1540
  1.3 1.0 %copy-start = (f32[32,8,2,256]{3,2,1,0:T(2,128)S(1)}, f32[32,8,2,256]{3,2,1,0:T(2,128)}, u32[]{:S(2)}) copy-start(f32[32,8,2,256]{3,2,1,0:T(2,128)} %param.14) | copy-start | bytes 1572868
  2.4 0.9 %copy-start.1 = (bf16[32,8,2,256]{3,2,1,0:T(2,128)(2,1)S(1)}, bf16[32,8,2,256]{3,2,1,0:T(2,128)(2,1)}, u32[]{:S(2)}) copy-start(bf16[32,8,2,256]{3,2,1,0:T(2,128)(2,1)} %param.13) | copy-start | bytes 786436
  3.3 0.9 %copy-start.4 = (bf16[128,945]{0,1:T(8,128)(2,1)S(1)}, bf16[128,945]{0,1:T(8,128)(2,1)}, u32[]{:S(2)}) copy-start(bf16[128,945]{0,1:T(8,128)(2,1)} %param.15) | copy-start | bytes 725764
  4.3 0.8 %copy-start.8 = (f32[3,8,2,256]{3,2,1,0:T(2,128)S(1)}, f32[3,8,2,256]{3,2,1,0:T(2,128)}, u32[]{:S(2)}) copy-start(f32[3,8,2,256]{3,2,1,0:T(2,128)} %param.12) | copy-start | bytes 147460
  5.1 25.5 %copy-start.2 = (bf16[2,256,256]{2,1,0:T(8,128)(2,1)S(1)}, bf16[2,256,256]{2,1,0:T(8,128)(2,1)}, u32[]{:S(2)}) copy-start(bf16[2,256,256]{2,1,0:T(8,128)(2,1)} %constant.13.clone.xi_ref) | copy-start | bytes 786436
  5.1 25.5 %copy-start.3 = (bf16[2,256,256]{2,1,0:T(8,128)(2,1)S(1)}, bf16[2,256,256]{2,1,0:T(8,128)(2,1)}, u32[]{:S(2)}) copy-start(bf16[2,256,256]{2,1,0:T(8,128)(2,1)} %constant.12.clone.xf_ref) | copy-start | bytes 786436
  5.1 25.6 %copy-start.5 = (bf16[2,256,128]{2,1,0:T(8,128)(2,1)S(1)}, bf16[2,256,128]{2,1,0:T(8,128)(2,1)}, u32[]{:S(2)}) copy-start(bf16[2,256,128]{2,1,0:T(8,128)(2,1)} %constant.15.clone.yi_ref) | copy-start | bytes 393220
  5.1 25.6 %copy-start.6 = (bf16[2,256,128]{2,1,0:T(8,128)(2,1)S(1)}, bf16[2,256,128]{2,1,0:T(8,128)(2,1)}, u32[]{:S(2)}) copy-start(bf16[2,256,128]{2,1,0:T(8,128)(2,1)} %constant.14.clone.yf_ref) | copy-start | bytes 393220
  5.1 25.6 %copy-start.7 = (bf16[2,128,64]{2,1,0:T(8,128)(2,1)S(1)}, bf16[2,128,64]{2,1,0:T(8,128)(2,1)}, u32[]{:S(2)}) copy-start(bf16[2,128,64]{2,1,0:T(8,128)(2,1)} %constant.17.clone.zi_ref) | copy-start | bytes 98308
  5.1 25.6 %copy-start.9 = (bf16[2,64,128]{2,1,0:T(8,128)(2,1)S(1)}, bf16[2,64,128]{2,1,0:T(8,128)(2,1)}, u32[]{:S(2)}) copy-start(bf16[2,64,128]{2,1,0:T(8,128)(2,1)} %constant.16.clone.zf_ref) | copy-start | bytes 98308
where the time goes:
time: 62.1 us; the launch traced here: 61.9 us
  Pallas kernels  54.6 us (88%)
  local copies, waits for them, and re-layouts  6.54 us (11%)
  between operations  0.74 us (1%)
    pallas_call x1, Pallas kernels, per_device(): pl.pallas_call(spectral_kernel, out_shape=jax.ShapeDtypeStruct((96, 128),...  29.1 us
    pallas_call x1, Pallas kernels, per_device(): pl.pallas_call(conv_kernel, out_shape=(jax.ShapeDtypeStruct((1024, 128),...  25.5 us
    unnamed x27, local copies, waits for them, and re-layouts  6.54 us

commit v1 on v0

--- a/solution.py
+++ b/solution.py
@@ -20,7 +20,10 @@
 def halves(table):
     high = table.astype(np.float32).astype(jnp.bfloat16)
     low = (table - high.astype(np.float64)).astype(np.float32).astype(jnp.bfloat16)
-    return np.stack([np.asarray(high), np.asarray(low)])
+    pair = np.stack([np.asarray(high), np.asarray(low)])
+    if table.shape[1] == 256:
+        pair = pair.reshape(2, -1, 2, 128).transpose(0, 2, 1, 3)
+    return np.ascontiguousarray(pair)
 
 
 def signed_waves(total):
@@ -83,7 +86,14 @@
     return jnp.dot(a, b, preferred_element_type=F32)
 
 
+def whole(table):
+    if len(table.shape) == 3:
+        return [table[0], table[1]]
+    return [jnp.concatenate([table[part, 0], table[part, 1]], 1) for part in range(2)]
+
+
 def data_by_table(value, table):
+    table = whole(table)
     high, low = split(value)
     return dot(high, table[0]) + (dot(low, table[0]) + dot(high, table[1]))
 
@@ -195,18 +205,9 @@
     return lax.rem(index + step + RANKS, RANKS)
 
 
-def spectral_kernel(
-    u_ref, xf_ref, xi_ref, yf_ref, yi_ref, zf_ref, zi_ref, out_ref, send, recv, send_sem, recv_sem
-):
+def project(u_ref, tables, out_ref, send, recv, send_sem, recv_sem):
     gy, gz = lax.axis_index("gy"), lax.axis_index("gz")
-    barrier = pltpu.get_barrier_semaphore()
-
-    def greet(d, carry):
-        pl.semaphore_signal(barrier, inc=1, device_id=(around(gy, d), gz), device_id_type=MESH)
-        pl.semaphore_signal(barrier, inc=1, device_id=(gy, around(gz, d)), device_id_type=MESH)
-        return carry
-
-    lax.fori_loop(1, RANKS, greet, 0)
+    xf_ref, xi_ref, yf_ref, yi_ref, zf_ref, zi_ref = tables
 
     def exchange(step, along_y):
         me = gy if along_y else gz
@@ -232,7 +233,6 @@
     tiles = x_forward(u_ref[...], xf_ref)
     for j in range(RANKS):
         send[0, j] = tiles[j]
-    pl.semaphore_wait(barrier, 2 * (RANKS - 1))
     exchange(0, True)
     tiles = y_forward(recv[0].reshape(128, 128), yf_ref)
     for j in range(RANKS):
@@ -256,16 +256,30 @@
         pltpu.make_async_copy(some, some, send_sem.at[step]).wait()
 
 
-def conv_kernel(
-    vel_hbm, hid_hbm, cell_hbm, weight_hbm, bias_ref, dec_ref, hid_out, cell_out, u_ref,
-    hid_in, hid_f, vel_f, cell_v, weight_v, weight_f, block_f, wide, side, slabs, vels, vel_t,
-    vz_s, vz_r, vy_s, vy_r, vc_s, vc_r, acc, moved, load_sem, send_sem, recv_sem, store_sem,
+def step_kernel(
+    vel_hbm, hid_hbm, cell_hbm, weight_hbm, bias_hbm, dec_hbm, *refs,
 ):
+    tables_hbm, (hid_out, cell_out, vel_out) = refs[:6], refs[6:9]
+    tables, refs = refs[9:15], refs[15:]
+    (
+        bias_ref, dec_ref, u_ref, vel_next,
+        hid_in, hid_f, vel_f, cell_v, weight_v, weight_f, block_f, wide, side, slabs, vels, vel_t,
+        vz_s, vz_r, vy_s, vy_r, vc_s, vc_r, acc, moved, send, recv,
+        load_sem, send_sem, recv_sem, store_sem, tile_send_sem, tile_recv_sem,
+    ) = refs
     gy, gz = lax.axis_index("gy"), lax.axis_index("gz")
     loads = [
         pltpu.make_async_copy(src, dst, load_sem.at[i])
         for i, (src, dst) in enumerate(
-            [(hid_hbm, hid_in), (vel_hbm, vel_f), (weight_hbm, weight_v), (cell_hbm, cell_v)]
+            [
+                (hid_hbm, hid_in),
+                (vel_hbm, vel_f),
+                (weight_hbm, weight_v),
+                (cell_hbm, cell_v),
+                (bias_hbm, bias_ref),
+                (dec_hbm, dec_ref),
+                *zip(tables_hbm, tables),
+            ]
         )
     ]
     for load in loads:
@@ -274,6 +288,13 @@
     targets = [(around(gy, sy), around(gz, sz)) for sy, sz in HALO]
     for target in targets:
         pl.semaphore_signal(barrier, inc=1, device_id=target, device_id_type=MESH)
+
+    def greet(d, carry):
+        pl.semaphore_signal(barrier, inc=1, device_id=(around(gy, d), gz), device_id_type=MESH)
+        pl.semaphore_signal(barrier, inc=1, device_id=(gy, around(gz, d)), device_id_type=MESH)
+        return carry
+
+    lax.fori_loop(2, RANKS - 1, greet, 0)
     vels[...] = jnp.zeros_like(vels)
 
     loads[0].wait()
@@ -302,7 +323,7 @@
             rows = jnp.concatenate([vels[y, z + 1], jnp.zeros((8, NX), F32)], 0)
             vc_s[2 * k + z] = rows.astype(BF16)
 
-    pl.semaphore_wait(barrier, len(HALO))
+    pl.semaphore_wait(barrier, len(HALO) + 2 * (RANKS - 3))
     copies = []
     for i, (sy, sz) in enumerate(HALO):
         k, z = (1 + sy) // 2, (1 + sz) // 2
@@ -349,6 +370,7 @@
     lax.fori_loop(1, 9, fill_own, 0)
 
     loads[2].wait()
+    loads[4].wait()
     weight_f[0:945, :] = weight_v[...].astype(F32)
     block_f[96:128, :] = jnp.zeros((32, 128), F32)
     for dy in range(3):
@@ -421,6 +443,7 @@
     lax.fori_loop(0, 10, fill_outer, 0)
 
     loads[3].wait()
+    loads[5].wait()
 
     def sigmoid(value):
         return 0.5 * jnp.tanh(0.5 * value) + 0.5
@@ -459,11 +482,26 @@
     hid_in[...] = hid_f[...].astype(BF16)
     hid_store = pltpu.make_async_copy(hid_in, hid_out, store_sem.at[1])
     hid_store.start()
+    for load in loads[6:]:
+        load.wait()
+    project(u_ref, tables, vel_next, send, recv, tile_send_sem, tile_recv_sem)
+    vel_store = pltpu.make_async_copy(vel_next, vel_out, store_sem.at[2])
+    vel_store.start()
     for pair in copies:
         for copy in pair:
             copy.wait_send()
     cell_store.wait()
     hid_store.wait()
+    vel_store.wait()
+
+
+def hand_on_kernel(*refs):
+    sources, results, sem = refs[:3], refs[3:6], refs[6]
+    copies = [pltpu.make_async_copy(a, b, sem.at[i]) for i, (a, b) in enumerate(zip(sources, results))]
+    for copy in copies:
+        copy.start()
+    for copy in copies:
+        copy.wait()
 
 
 def to_rows(array):
@@ -477,18 +515,24 @@
 
 
 def per_device(velocity, hidden, cell, gate_weight, gate_bias, decoder):
-    vmem = pl.BlockSpec(memory_space=pltpu.VMEM)
     anywhere = pl.BlockSpec(memory_space=pl.ANY)
-    hid_next, cell_next, advanced = pl.pallas_call(
-        conv_kernel,
-        out_shape=(
-            jax.ShapeDtypeStruct((1024, 128), BF16),
-            jax.ShapeDtypeStruct((1024, 128), F32),
-            jax.ShapeDtypeStruct((48, 256), F32),
-        ),
-        in_specs=[anywhere] * 4 + [vmem] * 2,
-        out_specs=(anywhere, anywhere, vmem),
+    tables = [halves(t) for t in (*x_tables(), *y_tables(), *z_tables())]
+    results = (
+        jax.ShapeDtypeStruct((1024, 128), BF16),
+        jax.ShapeDtypeStruct((1024, 128), F32),
+        jax.ShapeDtypeStruct((96, 128), F32),
+    )
+    outs = pl.pallas_call(
+        step_kernel,
+        out_shape=results,
+        in_specs=[anywhere] * 12,
+        out_specs=(anywhere,) * 3,
         scratch_shapes=[
+            *(pltpu.VMEM(t.shape, BF16) for t in tables),
+            pltpu.VMEM((1, 128), F32),
+            pltpu.VMEM((3, 32), BF16),
+            pltpu.VMEM((48, 256), F32),
+            pltpu.VMEM((96, 128), F32),
             pltpu.VMEM((1024, 128), BF16),
             pltpu.VMEM((1024, 128), F32),
             pltpu.VMEM((96, 128), F32),
@@ -509,13 +553,17 @@
             pltpu.VMEM((4, 16, NX), BF16),
             pltpu.VMEM((8, 256, 256), F32),
             pltpu.VMEM((2, 128, 128), F32),
-            pltpu.SemaphoreType.DMA((4,)),
+            pltpu.VMEM((4, RANKS, 8, 128), F32),
+            pltpu.VMEM((4, RANKS, 8, 128), F32),
+            pltpu.SemaphoreType.DMA((12,)),
             pltpu.SemaphoreType.DMA((8, 2)),
             pltpu.SemaphoreType.DMA((8, 2)),
-            pltpu.SemaphoreType.DMA((2,)),
+            pltpu.SemaphoreType.DMA((3,)),
+            pltpu.SemaphoreType.DMA((4,)),
+            pltpu.SemaphoreType.DMA((4,)),
         ],
         compiler_params=pltpu.CompilerParams(
-            collective_id=0, has_side_effects=True, vmem_limit_bytes=24 * 1024 * 1024
+            collective_id=0, has_side_effects=True, vmem_limit_bytes=56 * 1024 * 1024
         ),
     )(
         to_rows(velocity),
@@ -524,24 +572,17 @@
         gate_weight.T,
         gate_bias.reshape(1, 128),
         decoder,
+        *(jnp.asarray(t) for t in tables),
     )
-    tables = [jnp.asarray(halves(t)) for t in (*x_tables(), *y_tables(), *z_tables())]
-    velocity_next = pl.pallas_call(
-        spectral_kernel,
-        out_shape=jax.ShapeDtypeStruct((96, 128), F32),
-        in_specs=[vmem] * 7,
-        out_specs=vmem,
-        scratch_shapes=[
-            pltpu.VMEM((4, RANKS, 8, 128), F32),
-            pltpu.VMEM((4, RANKS, 8, 128), F32),
-            pltpu.SemaphoreType.DMA((4,)),
-            pltpu.SemaphoreType.DMA((4,)),
-        ],
-        compiler_params=pltpu.CompilerParams(
-            collective_id=1, has_side_effects=True, vmem_limit_bytes=16 * 1024 * 1024
-        ),
-    )(advanced, *tables)
-    return from_rows(hid_next), from_rows(cell_next), from_rows(velocity_next)
+    outs = pl.pallas_call(
+        hand_on_kernel,
+        out_shape=results,
+        in_specs=[anywhere] * 3,
+        out_specs=(anywhere,) * 3,
+        scratch_shapes=[pltpu.SemaphoreType.DMA((3,))],
+        compiler_params=pltpu.CompilerParams(vmem_limit_bytes=56 * 1024 * 1024),
+    )(*outs)
+    return tuple(from_rows(out) for out in outs)
 
 
 def solution(mesh):

time: 62.1 us -> 80.9 us (1.30)
  Pallas kernels: 54.6 us -> 80.2 us
  local copies, waits for them, and re-layouts: 6.54 us -> 0 us
    pallas_call x2, Pallas kernels: 54.6 us -> 80.2 us  [the longest x1 53.8 us: per_device(): pl.pallas_call(step_kernel, out_shape=results, in_specs=[anywhere] * 12,...]
    unnamed x27 -> x0, local copies, waits for them, and re-layouts: 6.54 us -> none
where the time goes in v1:
time: 80.9 us; the launch traced here: 80.8 us
  Pallas kernels  80.2 us (99%)
    pallas_call x1, Pallas kernels, per_device(): pl.pallas_call(step_kernel, out_shape=results, in_specs=[anywhere] * 12,...  53.8 us
    pallas_call x1, Pallas kernels, per_device(): pl.pallas_call(hand_on_kernel, out_shape=results, in_specs=[anywhere] * 3...  26.4 us

profile of v1, /device:TPU:1, one launch (start us, length us, event | category | flops | bytes accessed | tf_op | source)
XLA Modules:
  0.0 80.8 jit_solution(12643710691679632562)
XLA Ops:
  0.6 53.8 %shard_map.139 = (bf16[1024,128]{1,0:T(8,128)(2,1)}, f32[1024,128]{1,0:T(8,128)}, f32[96,128]{1,0:T(8,128)}) custom-call(f32[96,128]{1,0:T(8,128)} %bitcast.35, bf16[1024,128]{1,0:T(8,128)(2,1)} %bitcast.33, f32[1024,128]{1,0:T(8,128)} %bitcast.32, bf16[945,128]{1,0:T(8,128)(2,1)} %bitcast.34, f32[1,128]{1,0:T(1,128)} %bitcast.36, bf16[3,32]{1,0:T(4,128)(2,1)} %dec_hbm.1, ...), custom_call_target="tpu_custom_call" | custom-call | tf_op jit(solution)/shard_map/pallas_call | solution.py:525
  54.4 26.4 %shard_map.140 = (bf16[1024,128]{1,0:T(8,128)(2,1)}, f32[1024,128]{1,0:T(8,128)}, f32[96,128]{1,0:T(8,128)}) custom-call(bf16[1024,128]{1,0:T(8,128)(2,1)} %get-tuple-element.9.refs_0_, f32[1024,128]{1,0:T(8,128)} %get-tuple-element.10.refs_1_, f32[96,128]{1,0:T(8,128)} %get-tuple-element.11.refs_2_), custom_call_target="tpu_custom_call" | custom-call | tf_op jit(solution)/shard_map/pallas_call | solution.py:577

commit v2 on v1

--- a/solution.py
+++ b/solution.py
@@ -496,11 +496,15 @@
 
 
 def hand_on_kernel(*refs):
-    sources, results, sem = refs[:3], refs[3:6], refs[6]
-    copies = [pltpu.make_async_copy(a, b, sem.at[i]) for i, (a, b) in enumerate(zip(sources, results))]
-    for copy in copies:
+    sources, results, held, sem = refs[:3], refs[3:6], refs[6:9], refs[9]
+    arrive = [pltpu.make_async_copy(a, b, sem.at[0, i]) for i, (a, b) in enumerate(zip(sources, held))]
+    leave = [pltpu.make_async_copy(a, b, sem.at[1, i]) for i, (a, b) in enumerate(zip(held, results))]
+    for copy in arrive:
         copy.start()
-    for copy in copies:
+    for i in (2, 0, 1):
+        arrive[i].wait()
+        leave[i].start()
+    for copy in leave:
         copy.wait()
 
 
@@ -579,7 +583,7 @@
         out_shape=results,
         in_specs=[anywhere] * 3,
         out_specs=(anywhere,) * 3,
-        scratch_shapes=[pltpu.SemaphoreType.DMA((3,))],
+        scratch_shapes=[*(pltpu.VMEM(r.shape, r.dtype) for r in results), pltpu.SemaphoreType.DMA((2, 3))],
         compiler_params=pltpu.CompilerParams(vmem_limit_bytes=56 * 1024 * 1024),
     )(*outs)
     return tuple(from_rows(out) for out in outs)

time: 80.9 us -> 56.5 us (0.70)
  Pallas kernels: 80.2 us -> 55.7 us
    pallas_call x1, Pallas kernels: 26.4 us -> 1.98 us  [per_device(): pl.pallas_call(hand_on_kernel, out_shape=results, in_specs=[anywhere] * 3...]
where the time goes in v2:
time: 56.5 us; the launch traced here: 56.4 us
  Pallas kernels  55.7 us (99%)
  between operations  0.64 us (1%)
    pallas_call x1, Pallas kernels, per_device(): pl.pallas_call(step_kernel, out_shape=results, in_specs=[anywhere] * 12,...  53.8 us
    pallas_call x1, Pallas kernels, per_device(): pl.pallas_call(hand_on_kernel, out_shape=results, in_specs=[anywhere] * 3...  1.98 us

profile of v2, /device:TPU:1, one launch (start us, length us, event | category | flops | bytes accessed | tf_op | source)
XLA Modules:
  0.0 56.4 jit_solution(13207198413236487559)
XLA Ops:
  0.6 53.8 %shard_map.139 = (bf16[1024,128]{1,0:T(8,128)(2,1)}, f32[1024,128]{1,0:T(8,128)}, f32[96,128]{1,0:T(8,128)}) custom-call(f32[96,128]{1,0:T(8,128)} %bitcast.35, bf16[1024,128]{1,0:T(8,128)(2,1)} %bitcast.33, f32[1024,128]{1,0:T(8,128)} %bitcast.32, bf16[945,128]{1,0:T(8,128)(2,1)} %bitcast.34, f32[1,128]{1,0:T(1,128)} %bitcast.36, bf16[3,32]{1,0:T(4,128)(2,1)} %dec_hbm.1, ...), custom_call_target="tpu_custom_call" | custom-call | tf_op jit(solution)/shard_map/pallas_call | solution.py:529
  54.4 2.0 %shard_map.140 = (bf16[1024,128]{1,0:T(8,128)(2,1)}, f32[1024,128]{1,0:T(8,128)}, f32[96,128]{1,0:T(8,128)}) custom-call(bf16[1024,128]{1,0:T(8,128)(2,1)} %get-tuple-element.9.refs_0_, f32[1024,128]{1,0:T(8,128)} %get-tuple-element.10.refs_1_, f32[96,128]{1,0:T(8,128)} %get-tuple-element.11.refs_2_), custom_call_target="tpu_custom_call" | custom-call | tf_op jit(solution)/shard_map/pallas_call | solution.py:581

commit v3 on v2

--- a/solution.py
+++ b/solution.py
@@ -205,11 +205,11 @@
     return lax.rem(index + step + RANKS, RANKS)
 
 
-def project(u_ref, tables, out_ref, send, recv, send_sem, recv_sem):
+def project(u_ref, tables, out_ref, send, recv, send_sem, recv_sem, meanwhile):
     gy, gz = lax.axis_index("gy"), lax.axis_index("gz")
     xf_ref, xi_ref, yf_ref, yi_ref, zf_ref, zi_ref = tables
 
-    def exchange(step, along_y):
+    def exchange(step, along_y, meanwhile=None):
         me = gy if along_y else gz
 
         def start(d, carry):
@@ -227,13 +227,15 @@
 
         lax.fori_loop(1, RANKS, start, 0)
         recv[step, pl.ds(me, 1)] = send[step, pl.ds(me, 1)]
+        if meanwhile is not None:
+            meanwhile()
         some = recv.at[step, pl.ds(0, RANKS - 1)]
         pltpu.make_async_copy(some, some, recv_sem.at[step]).wait()
 
     tiles = x_forward(u_ref[...], xf_ref)
     for j in range(RANKS):
         send[0, j] = tiles[j]
-    exchange(0, True)
+    exchange(0, True, meanwhile)
     tiles = y_forward(recv[0].reshape(128, 128), yf_ref)
     for j in range(RANKS):
         send[1, j] = tiles[j]
@@ -264,7 +266,7 @@
     (
         bias_ref, dec_ref, u_ref, vel_next,
         hid_in, hid_f, vel_f, cell_v, weight_v, weight_f, block_f, wide, side, slabs, vels, vel_t,
-        vz_s, vz_r, vy_s, vy_r, vc_s, vc_r, acc, moved, send, recv,
+        vz_s, vz_r, vy_s, vy_r, vc_s, vc_r, acc, cells, hids, moved, send, recv,
         load_sem, send_sem, recv_sem, store_sem, tile_send_sem, tile_recv_sem,
     ) = refs
     gy, gz = lax.axis_index("gy"), lax.axis_index("gz")
@@ -324,34 +326,54 @@
             vc_s[2 * k + z] = rows.astype(BF16)
 
     pl.semaphore_wait(barrier, len(HALO) + 2 * (RANKS - 3))
-    copies = []
+    copies = {}
+
+    def start_halo(name, i, n, src, dst):
+        copies[name] = pltpu.make_async_remote_copy(
+            src_ref=src,
+            dst_ref=dst,
+            send_sem=send_sem.at[i, n],
+            recv_sem=recv_sem.at[i, n],
+            device_id=targets[i],
+            device_id_type=MESH,
+        )
+        copies[name].start()
+
+    mids = pl.ds(32, 32)
+
+    def send_plane(part):
+        for i, (sy, sz) in enumerate(HALO):
+            if sy == 0:
+                z = (1 + sz) // 2
+                ys = pl.ds(1 + 4 * part, 4)
+                src, dst = slabs.at[ys, z + 1, mids], slabs.at[ys, 3 - 3 * z, mids]
+                start_halo(("plane", z, part), i, part, src, dst)
+
+    def send_edge(i):
+        sy, sz = HALO[i]
+        k, z = (1 + sy) // 2, (1 + sz) // 2
+        if sz == 0:
+            src, dst = slabs.at[1 + 7 * k, pl.ds(1, 2), mids], slabs.at[9 - 9 * k, pl.ds(1, 2), mids]
+            start_halo(("edge", k, 0), i, 0, src, dst)
+            start_halo(("edge", k, 1), i, 1, vy_s.at[k], vy_r.at[k])
+        else:
+            src, dst = slabs.at[1 + 7 * k, 1 + z, mids], slabs.at[9 - 9 * k, 3 - 3 * z, mids]
+            start_halo(("corner", k, z, 0), i, 0, src, dst)
+            start_halo(("corner", k, z, 1), i, 1, vc_s.at[2 * k + z], vc_r.at[2 * k + z])
+
+    send_plane(0)
     for i, (sy, sz) in enumerate(HALO):
-        k, z = (1 + sy) // 2, (1 + sz) // 2
-        src_y, dst_y = (pl.ds(1, 8), pl.ds(1, 8)) if sy == 0 else (pl.ds(1 + 7 * k, 1), pl.ds(9 - 9 * k, 1))
-        src_z, dst_z = (pl.ds(1, 2), pl.ds(1, 2)) if sz == 0 else (pl.ds(1 + z, 1), pl.ds(3 - 3 * z, 1))
         if sy == 0:
-            extra = (vz_s.at[z], vz_r.at[z])
-        elif sz == 0:
-            extra = (vy_s.at[k], vy_r.at[k])
-        else:
-            extra = (vc_s.at[2 * k + z], vc_r.at[2 * k + z])
-        mids = pl.ds(32, 32)
-        pair = []
-        for n, (src, dst) in enumerate(
-            [(slabs.at[src_y, src_z, mids], slabs.at[dst_y, dst_z, mids]), extra]
-        ):
-            pair.append(
-                pltpu.make_async_remote_copy(
-                    src_ref=src,
-                    dst_ref=dst,
-                    send_sem=send_sem.at[i, n],
-                    recv_sem=recv_sem.at[i, n],
-                    device_id=targets[i],
-                    device_id_type=MESH,
-                )
-            )
-            pair[-1].start()
-        copies.append(pair)
+            z = (1 + sz) // 2
+            start_halo(("side", z), i, 2, vz_s.at[z], vz_r.at[z])
+    for wanted in ((1, True), (-1, False), (1, False)):
+        for i, (sy, sz) in enumerate(HALO):
+            if (sy, sz != 0) == wanted:
+                send_edge(i)
+    send_plane(1)
+    for i, (sy, sz) in enumerate(HALO):
+        if sy == -1 and sz != 0:
+            send_edge(i)
 
     def fill(y, z):
         mid = slabs[y, z, 32:64, :].astype(F32)
@@ -373,6 +395,8 @@
     loads[4].wait()
     weight_f[0:945, :] = weight_v[...].astype(F32)
     block_f[96:128, :] = jnp.zeros((32, 128), F32)
+    gate = lax.broadcasted_iota(jnp.int32, (128, 128), 0)
+    gate_scale = jnp.where((gate >= 64) & (gate < 96), 1.0, 0.5)
     for dy in range(3):
         for dz in range(3):
             first = (9 * dy + 3 * dz) * 35
@@ -387,7 +411,7 @@
                     high = rest.astype(BF16).astype(F32)
                     block_f[112 + part : 113 + part, :] = high
                     rest = rest - high
-            turned = block_f[...].T.astype(BF16)
+            turned = (block_f[...].T * gate_scale).astype(BF16)
             if dy == 1 and dz == 1:
                 block_f[112:120, :] = jnp.zeros((8, 128), F32)
             if dz == 0:
@@ -409,10 +433,22 @@
 
     lax.fori_loop(1, 7, inner_step, 0)
 
-    for i in (6, 7):
-        for copy in copies[i]:
-            copy.wait_recv()
-        k = (1 + HALO[i][0]) // 2
+    loads[3].wait()
+    loads[5].wait()
+
+    def own_cells(y, carry):
+        for z in range(2):
+            for t in range(2):
+                cells[y, z, :, 128 * t : 128 * t + 128] = cell_v[
+                    pl.ds(y * 4 + 2 * t + z, 32, stride=32), :
+                ]
+        return carry
+
+    lax.fori_loop(0, 8, own_cells, 0)
+
+    for k in range(2):
+        copies["edge", k, 0].wait_recv()
+        copies["edge", k, 1].wait_recv()
         rows = vy_r[k].astype(F32)
         y = 9 - 9 * k
         vels[y, 1] = rows[0:8]
@@ -422,54 +458,47 @@
     inner(0)
     inner(7)
 
-    for i in range(6):
-        for copy in copies[i]:
-            copy.wait_recv()
+    def update(y, carry):
+        for z in range(2):
+            outer = slabs[pl.ds(y, 3), 3 * z].reshape(3 * SLAB, NX)
+            gates = acc[y, 128 * z : 128 * z + 128, :] + dot(side[z], outer)
+            turned = jnp.tanh(gates)
+            new = 0.5 * (
+                (turned[32:64] + 1.0) * cells[y, z] + (turned[0:32] + 1.0) * turned[64:96]
+            )
+            cells[y, z] = new
+            hids[y, z] = (0.5 * (turned[96:128] + 1.0) * jnp.tanh(new)).astype(BF16)
+        return carry
+
+    def fill_outer(y, carry):
+        fill(y, 0)
+        fill(y, 3)
+        return carry
+
     for z in range(2):
+        copies["side", z].wait_recv()
         to = 3 - 3 * z
         rows = vz_r[z].astype(F32)
         for t in range(2):
             vel_t[t] = rows[:, 128 * t : 128 * t + 128]
             for y in range(8):
                 vels[y + 1, to, 0:3, 128 * t : 128 * t + 128] = vel_t[t, pl.ds(y, 3, stride=8), :]
-        for k in range(2):
-            vels[9 - 9 * k, to] = vc_r[2 * k + z].astype(F32)[0:8]
-
-    def fill_outer(y, carry):
-        fill(y, 0)
-        fill(y, 3)
-        return carry
-
-    lax.fori_loop(0, 10, fill_outer, 0)
-
-    loads[3].wait()
-    loads[5].wait()
-
-    def sigmoid(value):
-        return 0.5 * jnp.tanh(0.5 * value) + 0.5
-
-    def update(y, carry):
-        for z in range(2):
-            outer = slabs[pl.ds(y, 3), 3 * z].reshape(3 * SLAB, NX)
-            gates = acc[y, 128 * z : 128 * z + 128, :] + dot(side[z], outer)
-            hidden_parts = []
+    for part, ys, rows in ((0, (0, 5), (0, 3)), (1, (5, 10), (3, 8))):
+        k = 1 - part
+        for z in range(2):
+            copies["plane", z, part].wait_recv()
+            copies["corner", k, z, 0].wait_recv()
+            copies["corner", k, z, 1].wait_recv()
+            vels[9 - 9 * k, 3 - 3 * z] = vc_r[2 * k + z].astype(F32)[0:8]
+        lax.fori_loop(*ys, fill_outer, 0)
+        lax.fori_loop(*rows, update, 0)
+
+    for y in range(8):
+        for z in range(2):
+            advanced = vels[y + 1, z + 1, 0:3, :] + dot(dec_ref[...], hids[y, z])
             for t in range(2):
-                lanes = slice(128 * t, 128 * t + 128)
-                rows = pl.ds(y * 4 + 2 * t + z, 32, stride=32)
-                part = gates[:, lanes]
-                cell = sigmoid(part[32:64]) * cell_v[rows, :] + sigmoid(part[0:32]) * jnp.tanh(part[64:96])
-                hidden = sigmoid(part[96:128]) * jnp.tanh(cell)
-                cell_v[rows, :] = cell
-                hid_f[rows, :] = hidden
-                hidden_parts.append(hidden.astype(BF16))
-            increment = dot(dec_ref[...], jnp.concatenate(hidden_parts, 1))
-            advanced = vels[y + 1, z + 1, 0:3, :] + increment
-            for t in range(2):
-                rows = pl.ds(pl.multiple_of(16 * y + 8 * z, 8), 3)
-                moved[t, rows, :] = advanced[:, 128 * t : 128 * t + 128]
-        return carry
-
-    lax.fori_loop(0, 8, update, 0)
+                at = 16 * y + 8 * z
+                moved[t, at : at + 3, :] = advanced[:, 128 * t : 128 * t + 128]
     for c in range(3):
         for z in range(2):
             for t in range(2):
@@ -477,19 +506,32 @@
                 u_ref[start : start + 8, 128 * t : 128 * t + 128] = moved[
                     t, pl.ds(8 * z + c, 8, stride=16), :
                 ]
+
     cell_store = pltpu.make_async_copy(cell_v, cell_out, store_sem.at[0])
-    cell_store.start()
-    hid_in[...] = hid_f[...].astype(BF16)
     hid_store = pltpu.make_async_copy(hid_in, hid_out, store_sem.at[1])
-    hid_store.start()
+
+    def store_states():
+        def turn(y, carry):
+            for z in range(2):
+                for t in range(2):
+                    rows = pl.ds(y * 4 + 2 * t + z, 32, stride=32)
+                    lanes = slice(128 * t, 128 * t + 128)
+                    cell_v[rows, :] = cells[y, z, :, lanes]
+                    hid_f[rows, :] = hids[y, z, :, lanes].astype(F32)
+            return carry
+
+        lax.fori_loop(0, 8, turn, 0)
+        cell_store.start()
+        hid_in[...] = hid_f[...].astype(BF16)
+        hid_store.start()
+
     for load in loads[6:]:
         load.wait()
-    project(u_ref, tables, vel_next, send, recv, tile_send_sem, tile_recv_sem)
+    project(u_ref, tables, vel_next, send, recv, tile_send_sem, tile_recv_sem, store_states)
     vel_store = pltpu.make_async_copy(vel_next, vel_out, store_sem.at[2])
     vel_store.start()
-    for pair in copies:
-        for copy in pair:
-            copy.wait_send()
+    for copy in copies.values():
+        copy.wait_send()
     cell_store.wait()
     hid_store.wait()
     vel_store.wait()
@@ -556,12 +598,14 @@
             pltpu.VMEM((4, 16, NX), BF16),
             pltpu.VMEM((4, 16, NX), BF16),
             pltpu.VMEM((8, 256, 256), F32),
+            pltpu.VMEM((8, 2, 32, NX), F32),
+            pltpu.VMEM((8, 2, 32, NX), BF16),
             pltpu.VMEM((2, 128, 128), F32),
             pltpu.VMEM((4, RANKS, 8, 128), F32),
             pltpu.VMEM((4, RANKS, 8, 128), F32),
             pltpu.SemaphoreType.DMA((12,)),
-            pltpu.SemaphoreType.DMA((8, 2)),
-            pltpu.SemaphoreType.DMA((8, 2)),
+            pltpu.SemaphoreType.DMA((8, 3)),
+            pltpu.SemaphoreType.DMA((8, 3)),
             pltpu.SemaphoreType.DMA((3,)),
             pltpu.SemaphoreType.DMA((4,)),
             pltpu.SemaphoreType.DMA((4,)),

time: 56.5 us -> 53.1 us (0.940)
  Pallas kernels: 55.7 us -> 52.3 us
    pallas_call x1, Pallas kernels: 53.8 us -> 50.3 us  [per_device(): pl.pallas_call(step_kernel, out_shape=results, in_specs=[anywhere] * 12,...]
where the time goes in v3:
time: 53.1 us; the launch traced here: 52.9 us
  Pallas kernels  52.3 us (98%)
  between operations  0.64 us (1%)
    pallas_call x1, Pallas kernels, per_device(): pl.pallas_call(step_kernel, out_shape=results, in_specs=[anywhere] * 12,...  50.3 us
    pallas_call x1, Pallas kernels, per_device(): pl.pallas_call(hand_on_kernel, out_shape=results, in_specs=[anywhere] * 3...  1.98 us

profile of v3, /device:TPU:1, one launch (start us, length us, event | category | flops | bytes accessed | tf_op | source)
XLA Modules:
  0.0 52.9 jit_solution(13088627130163890206)
XLA Ops:
  0.6 50.3 %shard_map.139 = (bf16[1024,128]{1,0:T(8,128)(2,1)}, f32[1024,128]{1,0:T(8,128)}, f32[96,128]{1,0:T(8,128)}) custom-call(f32[96,128]{1,0:T(8,128)} %bitcast.35, bf16[1024,128]{1,0:T(8,128)(2,1)} %bitcast.33, f32[1024,128]{1,0:T(8,128)} %bitcast.32, bf16[945,128]{1,0:T(8,128)(2,1)} %bitcast.34, f32[1,128]{1,0:T(1,128)} %bitcast.36, bf16[3,32]{1,0:T(4,128)(2,1)} %dec_hbm.1, ...), custom_call_target="tpu_custom_call" | custom-call | tf_op jit(solution)/shard_map/pallas_call | solution.py:571
  50.9 2.0 %shard_map.140 = (bf16[1024,128]{1,0:T(8,128)(2,1)}, f32[1024,128]{1,0:T(8,128)}, f32[96,128]{1,0:T(8,128)}) custom-call(bf16[1024,128]{1,0:T(8,128)(2,1)} %get-tuple-element.9.refs_0_, f32[1024,128]{1,0:T(8,128)} %get-tuple-element.10.refs_1_, f32[96,128]{1,0:T(8,128)} %get-tuple-element.11.refs_2_), custom_call_target="tpu_custom_call" | custom-call | tf_op jit(solution)/shard_map/pallas_call | solution.py:625

commit v4 on v3

--- a/solution.py
+++ b/solution.py
@@ -26,55 +26,58 @@
     return np.ascontiguousarray(pair)
 
 
-def signed_waves(total):
-    index = np.arange(total)
-    wave = np.where(index < total // 2, index, index - total)
-    return np.where(index == total // 2, 0, wave).astype(np.float64)
-
-
 def x_tables():
-    lane = np.arange(128)
-    mode = (lane % 16) * 8 + lane // 16
+    mode = np.arange(128)
     n = np.arange(NX)
     angle = 2 * np.pi / NX * ((n[:, None] * mode[None, :]) % NX)
     sign = np.where(n % 2 == 0, 1.0, -1.0)
     imag = np.where(mode[None, :] == 0, sign[:, None], -np.sin(angle))
     forward = np.concatenate([np.cos(angle), imag], 1)
-    weight = np.where(mode == 0, 1.0, 2.0)
+    weight = np.where(mode == 0, 1.0, 2.0) / NX
     inverse = forward.T * np.concatenate([weight, weight])[:, None]
     return forward, inverse
 
 
+def real_waves(total):
+    half = total // 2
+    index = np.arange(total)
+    return np.where(index < half, index, index - half).astype(np.float64)
+
+
+def real_tables(total):
+    half = total // 2
+    cosines, sines = np.arange(half + 1), np.arange(1, half)
+    place = np.arange(total)
+    angle = 2 * np.pi / total * ((np.concatenate([cosines, sines])[:, None] * place[None, :]) % total)
+    is_sine = np.arange(total)[:, None] > half
+    analysis = np.where(is_sine, np.sin(angle), np.cos(angle))
+    weight = np.full(total, 2.0 / total)
+    weight[0] = weight[half] = 1.0 / total
+    synthesis = analysis.T * weight[None, :]
+    derivative = np.zeros((total, total))
+    for k in range(1, half):
+        derivative[k, half + k] = k
+        derivative[half + k, k] = -k
+    return analysis, synthesis, derivative
+
+
 def y_tables():
-    lane = np.arange(128)
-    mode = (lane % 16) * 8 + lane // 16
-    y = np.arange(NY)
-    angle = 2 * np.pi / NY * ((y[:, None] * mode[None, :]) % NY)
-    forward = np.concatenate([np.cos(angle), np.sin(angle)], 0)
-    inverse = np.concatenate([np.cos(angle).T, np.sin(angle).T], 0)
+    analysis, synthesis, derivative = real_tables(NY)
+    forward = np.concatenate([analysis, derivative @ analysis], 0)
+    inverse = np.concatenate([synthesis, -(synthesis @ derivative)], 0)
     return forward, inverse
 
 
 def z_tables():
-    kz = np.arange(NZ)
-    z = np.arange(NZ)
-    wave = signed_waves(NZ)[:, None]
-    angle = 2 * np.pi / NZ * ((kz[:, None] * z[None, :]) % NZ)
-    cosine, sine = np.cos(angle), np.sin(angle)
-    forward = np.zeros((2, NZ, RANKS, 2, 2, 2))
-    inverse = np.zeros((RANKS, 2, 2, 2, 2, NZ))
-    for own in range(2):
-        c, s = cosine[:, own::2], sine[:, own::2]
-        for field, scale in ((0, np.ones_like(wave)), (1, wave)):
-            forward[0, :, :, field, own, 0] = scale * c
-            forward[0, :, :, field, own, 1] = scale * s
-            forward[1, :, :, field, own, 1] = scale * c
-            forward[1, :, :, field, own, 0] = -scale * s
-            inverse[:, field, own, 0, 0, :] = (scale * c).T
-            inverse[:, field, own, 0, 1, :] = -(scale * s).T
-            inverse[:, field, own, 1, 1, :] = (scale * c).T
-            inverse[:, field, own, 1, 0, :] = (scale * s).T
-    return forward.reshape(64, 128), inverse.reshape(128, 64)
+    analysis, synthesis, derivative = real_tables(NZ)
+    lane = np.arange(NZ)
+    z = (lane // 8 % 2) * 16 + (lane % 4) * 4 + (lane // 4 % 2) * 2 + lane // 16
+    forward, inverse = np.zeros((128, 128)), np.zeros((128, 128))
+    for c in range(3):
+        lanes = slice(32 * c, 32 * c + 32)
+        forward[lanes, :32] = (derivative @ analysis if c == 2 else analysis)[:, z].T
+        inverse[:32, lanes] = (-(synthesis @ derivative) if c == 2 else synthesis)[z, :].T
+    return forward, inverse
 
 
 def split(value):
@@ -107,97 +110,67 @@
     return value if shift % 128 == 0 else pltpu.roll(value, shift % 128, 1)
 
 
-def roll_rows(value, shift):
-    return pltpu.roll(value, shift % value.shape[0], 0)
-
-
-def lane_ids():
-    return lax.broadcasted_iota(jnp.int32, (8, 128), 1)
-
-
-def lane_mix(values, count):
-    low = lane_ids() % 16
-    masks = [low == q for q in range(16)]
-    rolled = [roll_lanes(v, r) for r, v in enumerate(values)]
+def lane_mix(values, count, stride, base):
+    digit = lax.broadcasted_iota(jnp.int32, (8, 128), 1) // stride % base
+    masks = [digit == q for q in range(base)]
+    rolled = [roll_lanes(v, r * stride) for r, v in enumerate(values)]
     outs = []
     for j in range(count):
-        acc = jnp.zeros((8, 128), F32)
+        acc = rolled[0] if len(values) == base else jnp.zeros((8, 128), F32)
         for r, v in enumerate(rolled):
-            acc = jnp.where(masks[(j + r) % 16], v, acc)
-        outs.append(roll_lanes(acc, -j))
+            if r or len(values) < base:
+                acc = jnp.where(masks[(j + r) % base], v, acc)
+        outs.append(roll_lanes(acc, -j * stride))
     return outs
-
-
-def wave_of(index, total):
-    wave = jnp.where(index < total // 2, index, index - total)
-    return jnp.where(index == total // 2, 0, wave).astype(F32)
-
-
-def mode_waves(total):
-    lane = lane_ids()
-    return wave_of((lane % 16) * 8 + lane // 16, total)
 
 
 def x_forward(rows, table):
     spectrum = data_by_table(rows, table)
-    kx = mode_waves(2 * NX)
-
-    def part(c, z, p):
-        start = (2 * c + z) * 8
-        return spectrum[start : start + 8, 128 * p : 128 * p + 128]
-
     values = []
-    for c in (0, 2, 1):
-        for z in range(2):
-            for p in range(2):
-                values.append(part(c, z, p) * kx if c == 0 else part(c, z, p))
-    return lane_mix(values, RANKS)
-
-
-def swapped(value, sign):
-    even = lax.broadcasted_iota(jnp.int32, value.shape, 0) % 2 == 0
-    return jnp.where(even, sign * roll_rows(value, -1), -sign * roll_rows(value, 1))
-
-
-def y_forward(tiles, table):
-    rows = tiles.T
-    out = data_by_table(jnp.concatenate([rows, swapped(rows, 1.0)], 1), table)
-    ky = mode_waves(NY)
-    values = [out[16 * k : 16 * k + 8] + ky * out[16 * k + 8 : 16 * k + 16] for k in range(8)]
-    return lane_mix(values, RANKS)
-
-
-def z_both(tiles, forward, inverse, me_gy, me_gz):
-    numer = table_by_data(forward, tiles)
-    lane = lax.broadcasted_iota(jnp.int32, (NZ, 128), 1)
-    kx = (me_gy * 8 + lane % 8).astype(F32)
-    ky = wave_of(me_gz * 8 + lane // 16, NY)
-    kz = wave_of(lax.broadcasted_iota(jnp.int32, (NZ, 128), 0), NZ)
-    factor = (1.0 / (NX * NY * NZ)) / jnp.maximum(kx * kx + ky * ky + kz * kz, 1.0)
-    return table_by_data(inverse, numer * jnp.concatenate([factor, factor], 0))
-
-
-def y_inverse(tiles, table):
-    values = lane_mix(tiles, 8)
-    ky = mode_waves(NY)
+    for cz in range(6):
+        part = [spectrum[8 * cz : 8 * cz + 8, 128 * p : 128 * p + 128] for p in range(2)]
+        values += [-part[1], part[0]] if cz < 2 else part
+    return lane_mix(values, RANKS, 8, 16)
+
+
+def solve(tiles, yf_ref, yi_ref, zf_ref, zi_ref, wave_x):
+    def swap(blocks, first_of, second_of):
+        out = [None] * 16
+        for low in range(4):
+            mixed = lane_mix([blocks[first_of(low, i)] for i in range(4)], 4, 4, 4)
+            for i in range(4):
+                out[second_of(low, i)] = mixed[i]
+        return out
+
+    def by_source(low, i):
+        return (i // 2) * 8 + low * 2 + i % 2
+
+    def by_y(low, i):
+        return i * 4 + low
+
+    lane = lax.broadcasted_iota(jnp.int32, (NY, 128), 1)
+    is_y = (lane >= 32) & (lane < 64)
+    scale = jnp.where(lane < 32, wave_x, 1.0)
+    rows = jnp.concatenate(swap(tiles, by_source, by_y), 0)
+    out = table_by_data(yf_ref, rows)
+    terms = jnp.where(is_y, out[NY:], out[:NY]) * scale
+    divergence = data_by_table(terms, zf_ref)
+    row = lax.broadcasted_iota(jnp.int32, (NY, 128), 0)
+    wave_y = jnp.where(row < NY // 2, row, row - NY // 2).astype(F32)
+    wave_z = jnp.where(lane < NZ // 2, lane, lane - NZ // 2).astype(F32)
+    square = wave_x * wave_x + wave_y * wave_y + wave_z * wave_z
+    potential = divergence / jnp.maximum(square, 1.0)
+    out = table_by_data(yi_ref, data_by_table(potential, zi_ref))
+    rows = jnp.where(is_y, out[NY:], out[:NY]) * scale
+    return swap([rows[8 * i : 8 * i + 8] for i in range(16)], by_y, by_source)
+
+
+def x_inverse(tiles, table):
+    values = lane_mix(tiles, 12, 8, 16)
     rows = []
-    for v in values:
-        rows += [v, v * ky]
-    rows = jnp.concatenate(rows, 0)
-    out = data_by_table(jnp.concatenate([rows, swapped(rows, -1.0)], 1), table)
-    return out.T
-
-
-def x_inverse(tiles, table):
-    values = lane_mix(tiles, 12)
-    kx = mode_waves(2 * NX)
-    rows = []
-    for c, base in ((0, 0), (1, 8), (2, 4)):
-        for z in range(2):
-            pair = [values[base + 2 * z + p] for p in range(2)]
-            if c == 0:
-                pair = [v * kx for v in pair]
-            rows.append(jnp.concatenate(pair, 1))
+    for cz in range(6):
+        pair = values[2 * cz : 2 * cz + 2]
+        rows.append(jnp.concatenate([pair[1], -pair[0]] if cz < 2 else pair, 1))
     return data_by_table(jnp.concatenate(rows, 0), table)
 
 
@@ -205,22 +178,36 @@
     return lax.rem(index + step + RANKS, RANKS)
 
 
+def positions():
+    gy, gz = lax.axis_index("gy"), lax.axis_index("gz")
+    y, z_low, z_high, x, core = gy // 4, gy % 4, gz // 8, gz // 2 % 4, gz % 2
+
+    def first(index):
+        return (index // 4 * 4 + z_low, z_high * 8 + index % 4 * 2 + core)
+
+    def second(index):
+        return (y * 4 + index // 2 % 4, index // 8 * 8 + x * 2 + index % 2)
+
+    return (y * 4 + x, first), (z_high * 8 + z_low * 2 + core, second)
+
+
 def project(u_ref, tables, out_ref, send, recv, send_sem, recv_sem, meanwhile):
-    gy, gz = lax.axis_index("gy"), lax.axis_index("gz")
     xf_ref, xi_ref, yf_ref, yi_ref, zf_ref, zi_ref = tables
-
-    def exchange(step, along_y, meanwhile=None):
-        me = gy if along_y else gz
+    group_1, group_2 = positions()
+
+    def exchange(step, group, tiles, meanwhile=None):
+        me, place = group
+        for j in range(RANKS):
+            send[step, j] = tiles[j]
 
         def start(d, carry):
             to = around(me, d)
-            target = (to, gz) if along_y else (gy, to)
             pltpu.make_async_remote_copy(
                 src_ref=send.at[step, to],
                 dst_ref=recv.at[step, me],
                 send_sem=send_sem.at[step],
                 recv_sem=recv_sem.at[step],
-                device_id=target,
+                device_id=place(to),
                 device_id_type=MESH,
             ).start()
             return carry
@@ -231,20 +218,14 @@
             meanwhile()
         some = recv.at[step, pl.ds(0, RANKS - 1)]
         pltpu.make_async_copy(some, some, recv_sem.at[step]).wait()
-
-    tiles = x_forward(u_ref[...], xf_ref)
-    for j in range(RANKS):
-        send[0, j] = tiles[j]
-    exchange(0, True, meanwhile)
-    tiles = y_forward(recv[0].reshape(128, 128), yf_ref)
-    for j in range(RANKS):
-        send[1, j] = tiles[j]
-    exchange(1, False)
-    send[2] = z_both(recv[1].reshape(128, 128), zf_ref, zi_ref, gy, gz).reshape(RANKS, 8, 128)
-    exchange(2, False)
-    send[3] = y_inverse([recv[2, j] for j in range(RANKS)], yi_ref).reshape(RANKS, 8, 128)
-    exchange(3, True)
-    gradient = x_inverse([recv[3, j] for j in range(RANKS)], xi_ref)
+        return [recv[step, j] for j in range(RANKS)]
+
+    tiles = exchange(0, group_1, x_forward(u_ref[...], xf_ref), meanwhile)
+    tiles = exchange(1, group_2, lane_mix(tiles, RANKS, 1, 16))
+    wave_x = (group_1[0] * 8 + group_2[0] % 8).astype(F32)
+    tiles = exchange(2, group_2, solve(tiles, yf_ref, yi_ref, zf_ref, zi_ref, wave_x))
+    tiles = exchange(3, group_1, lane_mix(tiles, RANKS, 1, 16))
+    gradient = x_inverse(tiles, xi_ref)
     result = u_ref[...] - gradient
     for c in range(3):
         for z in range(2):
@@ -291,12 +272,14 @@
     for target in targets:
         pl.semaphore_signal(barrier, inc=1, device_id=target, device_id_type=MESH)
 
+    groups = positions()
+
     def greet(d, carry):
-        pl.semaphore_signal(barrier, inc=1, device_id=(around(gy, d), gz), device_id_type=MESH)
-        pl.semaphore_signal(barrier, inc=1, device_id=(gy, around(gz, d)), device_id_type=MESH)
+        for me, place in groups:
+            pl.semaphore_signal(barrier, inc=1, device_id=place(around(me, d)), device_id_type=MESH)
         return carry
 
-    lax.fori_loop(2, RANKS - 1, greet, 0)
+    lax.fori_loop(1, RANKS, greet, 0)
     vels[...] = jnp.zeros_like(vels)
 
     loads[0].wait()
@@ -325,7 +308,7 @@
             rows = jnp.concatenate([vels[y, z + 1], jnp.zeros((8, NX), F32)], 0)
             vc_s[2 * k + z] = rows.astype(BF16)
 
-    pl.semaphore_wait(barrier, len(HALO) + 2 * (RANKS - 3))
+    pl.semaphore_wait(barrier, len(HALO) + 2 * (RANKS - 1))
     copies = {}
 
     def start_halo(name, i, n, src, dst):

time: 53.1 us -> 49.8 us (0.938)
  Pallas kernels: 52.3 us -> 49.1 us
    pallas_call x1, Pallas kernels: 50.3 us -> 47.1 us  [per_device(): pl.pallas_call(step_kernel, out_shape=results, in_specs=[anywhere] * 12,...]
where the time goes in v4:
time: 49.8 us; the launch traced here: 49.7 us
  Pallas kernels  49.1 us (99%)
  between operations  0.64 us (1%)
    pallas_call x1, Pallas kernels, per_device(): pl.pallas_call(step_kernel, out_shape=results, in_specs=[anywhere] * 12,...  47.1 us
    pallas_call x1, Pallas kernels, per_device(): pl.pallas_call(hand_on_kernel, out_shape=results, in_specs=[anywhere] * 3...  1.98 us

profile of v4, /device:TPU:1, one launch (start us, length us, event | category | flops | bytes accessed | tf_op | source)
XLA Modules:
  0.0 49.7 jit_solution(12306974694786194640)
XLA Ops:
  0.6 47.1 %shard_map.139 = (bf16[1024,128]{1,0:T(8,128)(2,1)}, f32[1024,128]{1,0:T(8,128)}, f32[96,128]{1,0:T(8,128)}) custom-call(f32[96,128]{1,0:T(8,128)} %bitcast.35, bf16[1024,128]{1,0:T(8,128)(2,1)} %bitcast.33, f32[1024,128]{1,0:T(8,128)} %bitcast.32, bf16[945,128]{1,0:T(8,128)(2,1)} %bitcast.34, f32[1,128]{1,0:T(1,128)} %bitcast.36, bf16[3,32]{1,0:T(4,128)(2,1)} %dec_hbm.1, ...), custom_call_target="tpu_custom_call" | custom-call | tf_op jit(solution)/shard_map/pallas_call | solution.py:554
  47.7 2.0 %shard_map.140 = (bf16[1024,128]{1,0:T(8,128)(2,1)}, f32[1024,128]{1,0:T(8,128)}, f32[96,128]{1,0:T(8,128)}) custom-call(bf16[1024,128]{1,0:T(8,128)(2,1)} %get-tuple-element.9.refs_0_, f32[1024,128]{1,0:T(8,128)} %get-tuple-element.10.refs_1_, f32[96,128]{1,0:T(8,128)} %get-tuple-element.11.refs_2_), custom_call_target="tpu_custom_call" | custom-call | tf_op jit(solution)/shard_map/pallas_call | solution.py:608

commit v5 on v4

--- a/solution.py
+++ b/solution.py
@@ -242,13 +242,12 @@
 def step_kernel(
     vel_hbm, hid_hbm, cell_hbm, weight_hbm, bias_hbm, dec_hbm, *refs,
 ):
-    tables_hbm, (hid_out, cell_out, vel_out) = refs[:6], refs[6:9]
+    tables_hbm, (hid_in, cell_v, vel_next) = refs[:6], refs[6:9]
     tables, refs = refs[9:15], refs[15:]
     (
-        bias_ref, dec_ref, u_ref, vel_next,
-        hid_in, hid_f, vel_f, cell_v, weight_v, weight_f, block_f, wide, side, slabs, vels, vel_t,
+        bias_ref, dec_ref, u_ref, hid_f, vel_f, weight_v, weight_f, block_f, wide, side, slabs, vels, vel_t,
         vz_s, vz_r, vy_s, vy_r, vc_s, vc_r, acc, cells, hids, moved, send, recv,
-        load_sem, send_sem, recv_sem, store_sem, tile_send_sem, tile_recv_sem,
+        load_sem, send_sem, recv_sem, tile_send_sem, tile_recv_sem,
     ) = refs
     gy, gz = lax.axis_index("gy"), lax.axis_index("gz")
     loads = [
@@ -490,9 +489,6 @@
                     t, pl.ds(8 * z + c, 8, stride=16), :
                 ]
 
-    cell_store = pltpu.make_async_copy(cell_v, cell_out, store_sem.at[0])
-    hid_store = pltpu.make_async_copy(hid_in, hid_out, store_sem.at[1])
-
     def store_states():
         def turn(y, carry):
             for z in range(2):
@@ -504,32 +500,21 @@
             return carry
 
         lax.fori_loop(0, 8, turn, 0)
-        cell_store.start()
         hid_in[...] = hid_f[...].astype(BF16)
-        hid_store.start()
 
     for load in loads[6:]:
         load.wait()
     project(u_ref, tables, vel_next, send, recv, tile_send_sem, tile_recv_sem, store_states)
-    vel_store = pltpu.make_async_copy(vel_next, vel_out, store_sem.at[2])
-    vel_store.start()
     for copy in copies.values():
         copy.wait_send()
-    cell_store.wait()
-    hid_store.wait()
-    vel_store.wait()
 
 
 def hand_on_kernel(*refs):
-    sources, results, held, sem = refs[:3], refs[3:6], refs[6:9], refs[9]
-    arrive = [pltpu.make_async_copy(a, b, sem.at[0, i]) for i, (a, b) in enumerate(zip(sources, held))]
-    leave = [pltpu.make_async_copy(a, b, sem.at[1, i]) for i, (a, b) in enumerate(zip(held, results))]
-    for copy in arrive:
+    sources, results, sem = refs[:3], refs[3:6], refs[6]
+    copies = [pltpu.make_async_copy(a, b, sem.at[i]) for i, (a, b) in enumerate(zip(sources, results))]
+    for copy in copies:
         copy.start()
-    for i in (2, 0, 1):
-        arrive[i].wait()
-        leave[i].start()
-    for copy in leave:
+    for copy in copies:
         copy.wait()
 
 
@@ -545,6 +530,7 @@
 
 def per_device(velocity, hidden, cell, gate_weight, gate_bias, decoder):
     anywhere = pl.BlockSpec(memory_space=pl.ANY)
+    vmem = pl.BlockSpec(memory_space=pltpu.VMEM)
     tables = [halves(t) for t in (*x_tables(), *y_tables(), *z_tables())]
     results = (
         jax.ShapeDtypeStruct((1024, 128), BF16),
@@ -553,19 +539,16 @@
     )
     outs = pl.pallas_call(
         step_kernel,
-        out_shape=results,
+        out_shape=tuple(pltpu.VMEM(r.shape, r.dtype) for r in results),
         in_specs=[anywhere] * 12,
-        out_specs=(anywhere,) * 3,
+        out_specs=(vmem,) * 3,
         scratch_shapes=[
             *(pltpu.VMEM(t.shape, BF16) for t in tables),
             pltpu.VMEM((1, 128), F32),
             pltpu.VMEM((3, 32), BF16),
             pltpu.VMEM((48, 256), F32),
-            pltpu.VMEM((96, 128), F32),
-            pltpu.VMEM((1024, 128), BF16),
             pltpu.VMEM((1024, 128), F32),
             pltpu.VMEM((96, 128), F32),
-            pltpu.VMEM((1024, 128), F32),
             pltpu.VMEM((945, 128), BF16),
             pltpu.VMEM((952, 128), F32),
             pltpu.VMEM((128, 128), F32),
@@ -589,12 +572,11 @@
             pltpu.SemaphoreType.DMA((12,)),
             pltpu.SemaphoreType.DMA((8, 3)),
             pltpu.SemaphoreType.DMA((8, 3)),
-            pltpu.SemaphoreType.DMA((3,)),
             pltpu.SemaphoreType.DMA((4,)),
             pltpu.SemaphoreType.DMA((4,)),
         ],
         compiler_params=pltpu.CompilerParams(
-            collective_id=0, has_side_effects=True, vmem_limit_bytes=56 * 1024 * 1024
+            collective_id=0, has_side_effects=True, vmem_limit_bytes=58 * 1024 * 1024
         ),
     )(
         to_rows(velocity),
@@ -608,10 +590,10 @@
     outs = pl.pallas_call(
         hand_on_kernel,
         out_shape=results,
-        in_specs=[anywhere] * 3,
+        in_specs=[vmem] * 3,
         out_specs=(anywhere,) * 3,
-        scratch_shapes=[*(pltpu.VMEM(r.shape, r.dtype) for r in results), pltpu.SemaphoreType.DMA((2, 3))],
-        compiler_params=pltpu.CompilerParams(vmem_limit_bytes=56 * 1024 * 1024),
+        scratch_shapes=[pltpu.SemaphoreType.DMA((3,))],
+        compiler_params=pltpu.CompilerParams(vmem_limit_bytes=58 * 1024 * 1024),
     )(*outs)
     return tuple(from_rows(out) for out in outs)
 

time: 49.8 us -> 51.3 us (1.030)
  local copies, waits for them, and re-layouts: 0 us -> 2.09 us
  Pallas kernels: 49.1 us -> 48.5 us
    unnamed x0 -> x6, local copies, waits for them, and re-layouts: none -> 2.09 us
    pallas_call x2, Pallas kernels: 49.1 us -> 48.5 us  [the longest x1 46.5 us: per_device(): pl.pallas_call(step_kernel, out_shape=tuple((pltpu.VMEM(r.shape, r.dtype)...]
where the time goes in v5:
time: 51.3 us; the launch traced here: 51.2 us
  Pallas kernels  48.5 us (95%)
  local copies, waits for them, and re-layouts  2.09 us (4%)
  between operations  0.65 us (1%)
    pallas_call x1, Pallas kernels, per_device(): pl.pallas_call(step_kernel, out_shape=tuple((pltpu.VMEM(r.shape, r.dtype)...  46.5 us
    unnamed x6, local copies, waits for them, and re-layouts  2.09 us
    pallas_call x1, Pallas kernels, per_device(): pl.pallas_call(hand_on_kernel, out_shape=results, in_specs=[vmem] * 3, ou...  2.01 us

profile of v5, /device:TPU:1, one launch (start us, length us, event | category | flops | bytes accessed | tf_op | source)
XLA Modules:
  0.0 51.2 jit_solution(3890192728612961841)
XLA Ops:
  0.6 46.5 %shard_map.139 = (bf16[1024,128]{1,0:T(8,128)(2,1)S(1)}, f32[1024,128]{1,0:T(8,128)S(1)}, f32[96,128]{1,0:T(8,128)S(1)}) custom-call(f32[96,128]{1,0:T(8,128)} %bitcast.35, bf16[1024,128]{1,0:T(8,128)(2,1)} %bitcast.33, f32[1024,128]{1,0:T(8,128)} %bitcast.32, bf16[945,128]{1,0:T(8,128)(2,1)} %bitcast.34, f32[1,128]{1,0:T(1,128)} %bitcast.36, ...), custom_call_target="tpu_custom_call" | custom-call | tf_op jit(solution)/shard_map/pallas_call | solution.py:540
  47.1 0.0 copy-start
  47.1 0.8 %copy-done = f32[1024,128]{1,0:T(8,128)} copy-done((f32[1024,128]{1,0:T(8,128)}, f32[1024,128]{1,0:T(8,128)S(1)}, u32[]{:S(2)}) %copy-start) | copy-done | bytes 524312
  47.9 0.0 copy-start.1
  47.9 0.7 %copy-done.1 = bf16[1024,128]{1,0:T(8,128)(2,1)} copy-done((bf16[1024,128]{1,0:T(8,128)(2,1)}, bf16[1024,128]{1,0:T(8,128)(2,1)S(1)}, u32[]{:S(2)}) %copy-start.1) | copy-done | bytes 262168
  48.6 0.0 copy-start.2
  48.6 0.6 %copy-done.2 = f32[96,128]{1,0:T(8,128)} copy-done((f32[96,128]{1,0:T(8,128)}, f32[96,128]{1,0:T(8,128)S(1)}, u32[]{:S(2)}) %copy-start.2) | copy-done | bytes 49176
  49.2 2.0 %shard_map.140 = (bf16[1024,128]{1,0:T(8,128)(2,1)}, f32[1024,128]{1,0:T(8,128)}, f32[96,128]{1,0:T(8,128)}) custom-call(bf16[1024,128]{1,0:T(8,128)(2,1)} %copy-done.1, f32[1024,128]{1,0:T(8,128)} %copy-done, f32[96,128]{1,0:T(8,128)} %copy-done.2), custom_call_target="tpu_custom_call" | custom-call | tf_op jit(solution)/shard_map/pallas_call | solution.py:590
Async XLA Ops:
  47.1 0.8 %copy-start = (f32[1024,128]{1,0:T(8,128)}, f32[1024,128]{1,0:T(8,128)S(1)}, u32[]{:S(2)}) copy-start(f32[1024,128]{1,0:T(8,128)S(1)} %get-tuple-element.10.refs_1_) | copy-start | bytes 1572868
  47.9 0.7 %copy-start.1 = (bf16[1024,128]{1,0:T(8,128)(2,1)}, bf16[1024,128]{1,0:T(8,128)(2,1)S(1)}, u32[]{:S(2)}) copy-start(bf16[1024,128]{1,0:T(8,128)(2,1)S(1)} %get-tuple-element.9.refs_0_) | copy-start | bytes 786436
  48.6 0.6 %copy-start.2 = (f32[96,128]{1,0:T(8,128)}, f32[96,128]{1,0:T(8,128)S(1)}, u32[]{:S(2)}) copy-start(f32[96,128]{1,0:T(8,128)S(1)} %get-tuple-element.11.refs_2_) | copy-start | bytes 147460

commit v6 on v5

--- a/solution.py
+++ b/solution.py
@@ -593,7 +593,7 @@
         in_specs=[vmem] * 3,
         out_specs=(anywhere,) * 3,
         scratch_shapes=[pltpu.SemaphoreType.DMA((3,))],
-        compiler_params=pltpu.CompilerParams(vmem_limit_bytes=58 * 1024 * 1024),
+        compiler_params=pltpu.CompilerParams(vmem_limit_bytes=1024 * 1024),
     )(*outs)
     return tuple(from_rows(out) for out in outs)
 

time: 51.3 us -> 48.1 us (0.938)
  local copies, waits for them, and re-layouts: 2.09 us -> 0 us
  Pallas kernels: 48.5 us -> 47.4 us
    unnamed x6 -> x0, local copies, waits for them, and re-layouts: 2.09 us -> none
    pallas_call x1, Pallas kernels: 2.01 us -> 0.91 us  [per_device(): pl.pallas_call(hand_on_kernel, out_shape=results, in_specs=[vmem] * 3, ou...]
where the time goes in v6:
time: 48.1 us; the launch traced here: 48 us
  Pallas kernels  47.4 us (99%)
  between operations  0.64 us (1%)
    pallas_call x1, Pallas kernels, per_device(): pl.pallas_call(step_kernel, out_shape=tuple((pltpu.VMEM(r.shape, r.dtype)...  46.5 us

profile of v6, /device:TPU:1, one launch (start us, length us, event | category | flops | bytes accessed | tf_op | source)
XLA Modules:
  0.0 48.0 jit_solution(1667634470845406682)
XLA Ops:
  0.6 46.5 %shard_map.139 = (bf16[1024,128]{1,0:T(8,128)(2,1)S(1)}, f32[1024,128]{1,0:T(8,128)S(1)}, f32[96,128]{1,0:T(8,128)S(1)}) custom-call(f32[96,128]{1,0:T(8,128)} %bitcast.35, bf16[1024,128]{1,0:T(8,128)(2,1)} %bitcast.33, f32[1024,128]{1,0:T(8,128)} %bitcast.32, bf16[945,128]{1,0:T(8,128)(2,1)} %bitcast.34, f32[1,128]{1,0:T(1,128)} %bitcast.36, ...), custom_call_target="tpu_custom_call" | custom-call | tf_op jit(solution)/shard_map/pallas_call | solution.py:540
  47.1 0.9 %shard_map.140 = (bf16[1024,128]{1,0:T(8,128)(2,1)}, f32[1024,128]{1,0:T(8,128)}, f32[96,128]{1,0:T(8,128)}) custom-call(bf16[1024,128]{1,0:T(8,128)(2,1)S(1)} %get-tuple-element.9.refs_0_, f32[1024,128]{1,0:T(8,128)S(1)} %get-tuple-element.10.refs_1_, f32[96,128]{1,0:T(8,128)S(1)} %get-tuple-element.11.refs_2_), custom_call_target="tpu_custom_call" | custom-call | tf_op jit(solution)/shard_map/pallas_call | solution.py:590

commit v7 on v6

--- a/solution.py
+++ b/solution.py
@@ -200,7 +200,7 @@
         for j in range(RANKS):
             send[step, j] = tiles[j]
 
-        def start(d, carry):
+        for d in (8, 10, 9, 7, 6, 11, 5, 12, 4, 13, 3, 14, 2, 15, 1):
             to = around(me, d)
             pltpu.make_async_remote_copy(
                 src_ref=send.at[step, to],
@@ -210,9 +210,6 @@
                 device_id=place(to),
                 device_id_type=MESH,
             ).start()
-            return carry
-
-        lax.fori_loop(1, RANKS, start, 0)
         recv[step, pl.ds(me, 1)] = send[step, pl.ds(me, 1)]
         if meanwhile is not None:
             meanwhile()
@@ -264,7 +261,7 @@
             ]
         )
     ]
-    for load in loads:
+    for load in loads[:2]:
         load.start()
     barrier = pltpu.get_barrier_semaphore()
     targets = [(around(gy, sy), around(gz, sz)) for sy, sz in HALO]
@@ -327,7 +324,7 @@
         for i, (sy, sz) in enumerate(HALO):
             if sy == 0:
                 z = (1 + sz) // 2
-                ys = pl.ds(1 + 4 * part, 4)
+                ys = pl.ds(1 + 2 * part, 2)
                 src, dst = slabs.at[ys, z + 1, mids], slabs.at[ys, 3 - 3 * z, mids]
                 start_halo(("plane", z, part), i, part, src, dst)
 
@@ -347,20 +344,25 @@
     for i, (sy, sz) in enumerate(HALO):
         if sy == 0:
             z = (1 + sz) // 2
-            start_halo(("side", z), i, 2, vz_s.at[z], vz_r.at[z])
+            start_halo(("side", z), i, 4, vz_s.at[z], vz_r.at[z])
     for wanted in ((1, True), (-1, False), (1, False)):
         for i, (sy, sz) in enumerate(HALO):
             if (sy, sz != 0) == wanted:
                 send_edge(i)
     send_plane(1)
+    send_plane(2)
     for i, (sy, sz) in enumerate(HALO):
         if sy == -1 and sz != 0:
             send_edge(i)
+    send_plane(3)
+
+    for load in loads[2:]:
+        load.start()
 
     def fill(y, z):
-        mid = slabs[y, z, 32:64, :].astype(F32)
-        slabs[y, z, 0:32, :] = pltpu.roll(mid, 1, 1).astype(BF16)
-        slabs[y, z, 64:96, :] = pltpu.roll(mid, NX - 1, 1).astype(BF16)
+        mid = slabs[y, z, 32:64, :]
+        slabs[y, z, 0:32, :] = pltpu.roll(mid, 1, 1)
+        slabs[y, z, 64:96, :] = pltpu.roll(mid, NX - 1, 1)
         v = vels[y, z]
         first = v + pltpu.roll(pltpu.roll(v, 1, 1), 3, 0)
         tile = jnp.concatenate([first, pltpu.roll(v, NX - 1, 1), jnp.ones((16, NX), F32)], 0)
@@ -465,15 +467,20 @@
             vel_t[t] = rows[:, 128 * t : 128 * t + 128]
             for y in range(8):
                 vels[y + 1, to, 0:3, 128 * t : 128 * t + 128] = vel_t[t, pl.ds(y, 3, stride=8), :]
-    for part, ys, rows in ((0, (0, 5), (0, 3)), (1, (5, 10), (3, 8))):
-        k = 1 - part
+    for part, ys, rows in (
+        (0, (0, 3), (0, 1)), (1, (3, 5), (1, 3)), (2, (5, 7), (3, 5)), (3, (7, 10), (5, 8))
+    ):
         for z in range(2):
             copies["plane", z, part].wait_recv()
-            copies["corner", k, z, 0].wait_recv()
-            copies["corner", k, z, 1].wait_recv()
-            vels[9 - 9 * k, 3 - 3 * z] = vc_r[2 * k + z].astype(F32)[0:8]
-        lax.fori_loop(*ys, fill_outer, 0)
-        lax.fori_loop(*rows, update, 0)
+            if part in (0, 3):
+                k = 1 - part // 3
+                copies["corner", k, z, 0].wait_recv()
+                copies["corner", k, z, 1].wait_recv()
+                vels[9 - 9 * k, 3 - 3 * z] = vc_r[2 * k + z].astype(F32)[0:8]
+        for y in range(*ys):
+            fill_outer(y, 0)
+        for y in range(*rows):
+            update(y, 0)
 
     for y in range(8):
         for z in range(2):
@@ -570,8 +577,8 @@
             pltpu.VMEM((4, RANKS, 8, 128), F32),
             pltpu.VMEM((4, RANKS, 8, 128), F32),
             pltpu.SemaphoreType.DMA((12,)),
-            pltpu.SemaphoreType.DMA((8, 3)),
-            pltpu.SemaphoreType.DMA((8, 3)),
+            pltpu.SemaphoreType.DMA((8, 5)),
+            pltpu.SemaphoreType.DMA((8, 5)),
             pltpu.SemaphoreType.DMA((4,)),
             pltpu.SemaphoreType.DMA((4,)),
         ],

time: 48.1 us -> 46.1 us (0.958)
  Pallas kernels: 47.4 us -> 45.3 us
    pallas_call x1, Pallas kernels: 46.5 us -> 44.4 us  [per_device(): pl.pallas_call(step_kernel, out_shape=tuple((pltpu.VMEM(r.shape, r.dtype)...]
where the time goes in v7:
time: 46.1 us; the launch traced here: 45.9 us
  Pallas kernels  45.3 us (98%)
  between operations  0.64 us (1%)
    pallas_call x1, Pallas kernels, per_device(): pl.pallas_call(step_kernel, out_shape=tuple((pltpu.VMEM(r.shape, r.dtype)...  44.4 us

profile of v7, /device:TPU:1, one launch (start us, length us, event | category | flops | bytes accessed | tf_op | source)
XLA Modules:
  0.0 45.9 jit_solution(5882870244773145497)
XLA Ops:
  0.6 44.4 %shard_map.139 = (bf16[1024,128]{1,0:T(8,128)(2,1)S(1)}, f32[1024,128]{1,0:T(8,128)S(1)}, f32[96,128]{1,0:T(8,128)S(1)}) custom-call(f32[96,128]{1,0:T(8,128)} %bitcast.35, bf16[1024,128]{1,0:T(8,128)(2,1)} %bitcast.33, f32[1024,128]{1,0:T(8,128)} %bitcast.32, bf16[945,128]{1,0:T(8,128)(2,1)} %bitcast.34, f32[1,128]{1,0:T(1,128)} %bitcast.36, ...), custom_call_target="tpu_custom_call" | custom-call | tf_op jit(solution)/shard_map/pallas_call | solution.py:547
  45.0 0.9 %shard_map.140 = (bf16[1024,128]{1,0:T(8,128)(2,1)}, f32[1024,128]{1,0:T(8,128)}, f32[96,128]{1,0:T(8,128)}) custom-call(bf16[1024,128]{1,0:T(8,128)(2,1)S(1)} %get-tuple-element.9.refs_0_, f32[1024,128]{1,0:T(8,128)S(1)} %get-tuple-element.10.refs_1_, f32[96,128]{1,0:T(8,128)S(1)} %get-tuple-element.11.refs_2_), custom_call_target="tpu_custom_call" | custom-call | tf_op jit(solution)/shard_map/pallas_call | solution.py:597

commit v8 on v7

--- a/solution.py
+++ b/solution.py
@@ -178,6 +178,10 @@
     return lax.rem(index + step + RANKS, RANKS)
 
 
+def ring(step, length):
+    return min(step, length - step)
+
+
 def positions():
     gy, gz = lax.axis_index("gy"), lax.axis_index("gz")
     y, z_low, z_high, x, core = gy // 4, gy % 4, gz // 8, gz // 2 % 4, gz % 2
@@ -188,7 +192,16 @@
     def second(index):
         return (y * 4 + index // 2 % 4, index // 8 * 8 + x * 2 + index % 2)
 
-    return (y * 4 + x, first), (z_high * 8 + z_low * 2 + core, second)
+    z = z_high * 4 + z_low
+    first_others = [
+        lax.rem(y + dy, 4) * 4 + lax.rem(x + dx, 4)
+        for dy, dx in sorted(np.ndindex(4, 4), key=lambda d: -ring(d[0], 4) - ring(d[1], 4))[:-1]
+    ]
+    second_others = [
+        lax.rem(z + dz, 8) * 2 + lax.rem(core + dc, 2)
+        for dz, dc in sorted(np.ndindex(8, 2), key=lambda d: -ring(d[0], 8) - d[1])[:-1]
+    ]
+    return (y * 4 + x, first, first_others), (z * 2 + core, second, second_others)
 
 
 def project(u_ref, tables, out_ref, send, recv, send_sem, recv_sem, meanwhile):
@@ -196,12 +209,11 @@
     group_1, group_2 = positions()
 
     def exchange(step, group, tiles, meanwhile=None):
-        me, place = group
+        me, place, others = group
         for j in range(RANKS):
             send[step, j] = tiles[j]
 
-        for d in (8, 10, 9, 7, 6, 11, 5, 12, 4, 13, 3, 14, 2, 15, 1):
-            to = around(me, d)
+        for to in others:
             pltpu.make_async_remote_copy(
                 src_ref=send.at[step, to],
                 dst_ref=recv.at[step, me],
@@ -268,14 +280,9 @@
     for target in targets:
         pl.semaphore_signal(barrier, inc=1, device_id=target, device_id_type=MESH)
 
-    groups = positions()
-
-    def greet(d, carry):
-        for me, place in groups:
-            pl.semaphore_signal(barrier, inc=1, device_id=place(around(me, d)), device_id_type=MESH)
-        return carry
-
-    lax.fori_loop(1, RANKS, greet, 0)
+    for _, place, others in positions():
+        for to in others:
+            pl.semaphore_signal(barrier, inc=1, device_id=place(to), device_id_type=MESH)
     vels[...] = jnp.zeros_like(vels)
 
     loads[0].wait()

time: 46.1 us -> 45.7 us (level)
  no operation moved by 1% of the time
where the time goes in v8:
time: 45.7 us; the launch traced here: 45.5 us
  Pallas kernels  44.9 us (98%)
  between operations  0.64 us (1%)
    pallas_call x1, Pallas kernels, per_device(): pl.pallas_call(step_kernel, out_shape=tuple((pltpu.VMEM(r.shape, r.dtype)...  44 us

profile of v8, /device:TPU:1, one launch (start us, length us, event | category | flops | bytes accessed | tf_op | source)
XLA Modules:
  0.0 45.5 jit_solution(2396007354842182758)
XLA Ops:
  0.6 44.0 %shard_map.139 = (bf16[1024,128]{1,0:T(8,128)(2,1)S(1)}, f32[1024,128]{1,0:T(8,128)S(1)}, f32[96,128]{1,0:T(8,128)S(1)}) custom-call(f32[96,128]{1,0:T(8,128)} %bitcast.35, bf16[1024,128]{1,0:T(8,128)(2,1)} %bitcast.33, f32[1024,128]{1,0:T(8,128)} %bitcast.32, bf16[945,128]{1,0:T(8,128)(2,1)} %bitcast.34, f32[1,128]{1,0:T(1,128)} %bitcast.36, ...), custom_call_target="tpu_custom_call" | custom-call | tf_op jit(solution)/shard_map/pallas_call | solution.py:554
  44.6 0.9 %shard_map.140 = (bf16[1024,128]{1,0:T(8,128)(2,1)}, f32[1024,128]{1,0:T(8,128)}, f32[96,128]{1,0:T(8,128)}) custom-call(bf16[1024,128]{1,0:T(8,128)(2,1)S(1)} %get-tuple-element.9.refs_0_, f32[1024,128]{1,0:T(8,128)S(1)} %get-tuple-element.10.refs_1_, f32[96,128]{1,0:T(8,128)S(1)} %get-tuple-element.11.refs_2_), custom_call_target="tpu_custom_call" | custom-call | tf_op jit(solution)/shard_map/pallas_call | solution.py:604

commit v9 on v8

--- a/solution.py
+++ b/solution.py
@@ -264,7 +264,7 @@
         for i, (src, dst) in enumerate(
             [
                 (hid_hbm, hid_in),
-                (vel_hbm, vel_f),
+                (vel_hbm, vel_f.at[pl.ds(0, 96)]),
                 (weight_hbm, weight_v),
                 (cell_hbm, cell_v),
                 (bias_hbm, bias_ref),
@@ -300,16 +300,14 @@
 
     lax.fori_loop(0, 8, centre, 0)
     for z in range(2):
-        for t in range(2):
-            rows = vel_f[pl.ds(2 * t + z, 24, stride=4), :]
-            rows = jnp.concatenate([rows, jnp.zeros((8, 128), F32)], 0)
-            vz_s[z, :, 128 * t : 128 * t + 128] = rows.astype(BF16)
+        rows = [vel_f[pl.ds(2 * t + z, 24, stride=4), :] for t in range(2)]
+        vz_s[z] = jnp.concatenate(rows, 0).astype(BF16)
     for k in range(2):
         y = 1 + 7 * k
         vy_s[k] = jnp.concatenate([vels[y, 1], vels[y, 2]], 0).astype(BF16)
         for z in range(2):
-            rows = jnp.concatenate([vels[y, z + 1], jnp.zeros((8, NX), F32)], 0)
-            vc_s[2 * k + z] = rows.astype(BF16)
+            v = vels[y, z + 1]
+            vc_s[2 * k + z] = jnp.concatenate([v[:, :128], v[:, 128:]], 0).astype(BF16)
 
     pl.semaphore_wait(barrier, len(HALO) + 2 * (RANKS - 1))
     copies = {}
@@ -331,7 +329,7 @@
         for i, (sy, sz) in enumerate(HALO):
             if sy == 0:
                 z = (1 + sz) // 2
-                ys = pl.ds(1 + 2 * part, 2)
+                ys = pl.ds(*((1, 2), (3, 2), (5, 3), (8, 1))[part])
                 src, dst = slabs.at[ys, z + 1, mids], slabs.at[ys, 3 - 3 * z, mids]
                 start_halo(("plane", z, part), i, part, src, dst)
 
@@ -352,11 +350,13 @@
         if sy == 0:
             z = (1 + sz) // 2
             start_halo(("side", z), i, 4, vz_s.at[z], vz_r.at[z])
-    for wanted in ((1, True), (-1, False), (1, False)):
+    for wanted in ((1, True),):
         for i, (sy, sz) in enumerate(HALO):
             if (sy, sz != 0) == wanted:
                 send_edge(i)
     send_plane(1)
+    send_edge(6)
+    send_edge(7)
     send_plane(2)
     for i, (sy, sz) in enumerate(HALO):
         if sy == -1 and sz != 0:
@@ -471,11 +471,11 @@
         to = 3 - 3 * z
         rows = vz_r[z].astype(F32)
         for t in range(2):
-            vel_t[t] = rows[:, 128 * t : 128 * t + 128]
+            vel_t[t, 0:24] = rows[24 * t : 24 * t + 24]
             for y in range(8):
                 vels[y + 1, to, 0:3, 128 * t : 128 * t + 128] = vel_t[t, pl.ds(y, 3, stride=8), :]
     for part, ys, rows in (
-        (0, (0, 3), (0, 1)), (1, (3, 5), (1, 3)), (2, (5, 7), (3, 5)), (3, (7, 10), (5, 8))
+        (0, (0, 3), (0, 1)), (1, (3, 5), (1, 3)), (2, (5, 8), (3, 6)), (3, (8, 10), (6, 8))
     ):
         for z in range(2):
             copies["plane", z, part].wait_recv()
@@ -483,7 +483,8 @@
                 k = 1 - part // 3
                 copies["corner", k, z, 0].wait_recv()
                 copies["corner", k, z, 1].wait_recv()
-                vels[9 - 9 * k, 3 - 3 * z] = vc_r[2 * k + z].astype(F32)[0:8]
+                rows_c = vc_r[2 * k + z].astype(F32)
+                vels[9 - 9 * k, 3 - 3 * z] = jnp.concatenate([rows_c[0:8], rows_c[8:16]], 1)
         for y in range(*ys):
             fill_outer(y, 0)
         for y in range(*rows):
@@ -562,7 +563,7 @@
             pltpu.VMEM((3, 32), BF16),
             pltpu.VMEM((48, 256), F32),
             pltpu.VMEM((1024, 128), F32),
-            pltpu.VMEM((96, 128), F32),
+            pltpu.VMEM((256, 128), F32),
             pltpu.VMEM((945, 128), BF16),
             pltpu.VMEM((952, 128), F32),
             pltpu.VMEM((128, 128), F32),
@@ -570,13 +571,13 @@
             pltpu.VMEM((2, 128, 384), BF16),
             pltpu.VMEM((10, 4, SLAB, NX), BF16),
             pltpu.VMEM((10, 4, 8, NX), F32),
-            pltpu.VMEM((2, 32, 128), F32),
-            pltpu.VMEM((2, 32, NX), BF16),
-            pltpu.VMEM((2, 32, NX), BF16),
+            pltpu.VMEM((2, 64, 128), F32),
+            pltpu.VMEM((2, 48, 128), BF16),
+            pltpu.VMEM((2, 48, 128), BF16),
             pltpu.VMEM((2, 16, NX), BF16),
             pltpu.VMEM((2, 16, NX), BF16),
-            pltpu.VMEM((4, 16, NX), BF16),
-            pltpu.VMEM((4, 16, NX), BF16),
+            pltpu.VMEM((4, 16, 128), BF16),
+            pltpu.VMEM((4, 16, 128), BF16),
             pltpu.VMEM((8, 256, 256), F32),
             pltpu.VMEM((8, 2, 32, NX), F32),
             pltpu.VMEM((8, 2, 32, NX), BF16),

time: 45.7 us -> 45.2 us (0.989)
  no operation moved by 1% of the time
where the time goes in v9:
time: 45.2 us; the launch traced here: 45.1 us
  Pallas kernels  44.5 us (98%)
  between operations  0.64 us (1%)
    pallas_call x1, Pallas kernels, per_device(): pl.pallas_call(step_kernel, out_shape=tuple((pltpu.VMEM(r.shape, r.dtype)...  43.6 us
    pallas_call x1, Pallas kernels, per_device(): pl.pallas_call(hand_on_kernel, out_shape=results, in_specs=[vmem] * 3, ou...  0.91 us

profile of v9, /device:TPU:1, one launch (start us, length us, event | category | flops | bytes accessed | tf_op | source)
XLA Modules:
  0.0 45.1 jit_solution(10464907076821632880)
XLA Ops:
  0.6 43.6 %shard_map.139 = (bf16[1024,128]{1,0:T(8,128)(2,1)S(1)}, f32[1024,128]{1,0:T(8,128)S(1)}, f32[96,128]{1,0:T(8,128)S(1)}) custom-call(f32[96,128]{1,0:T(8,128)} %bitcast.35, bf16[1024,128]{1,0:T(8,128)(2,1)} %bitcast.33, f32[1024,128]{1,0:T(8,128)} %bitcast.32, bf16[945,128]{1,0:T(8,128)(2,1)} %bitcast.34, f32[1,128]{1,0:T(1,128)} %bitcast.36, ...), custom_call_target="tpu_custom_call" | custom-call | tf_op jit(solution)/shard_map/pallas_call | solution.py:555
  44.2 0.9 %shard_map.140 = (bf16[1024,128]{1,0:T(8,128)(2,1)}, f32[1024,128]{1,0:T(8,128)}, f32[96,128]{1,0:T(8,128)}) custom-call(bf16[1024,128]{1,0:T(8,128)(2,1)S(1)} %get-tuple-element.9.refs_0_, f32[1024,128]{1,0:T(8,128)S(1)} %get-tuple-element.10.refs_1_, f32[96,128]{1,0:T(8,128)S(1)} %get-tuple-element.11.refs_2_), custom_call_target="tpu_custom_call" | custom-call | tf_op jit(solution)/shard_map/pallas_call | solution.py:605

commit v10 on v9

--- a/solution.py
+++ b/solution.py
@@ -208,6 +208,10 @@
     xf_ref, xi_ref, yf_ref, yi_ref, zf_ref, zi_ref = tables
     group_1, group_2 = positions()
 
+    def sent(step):
+        some = send.at[step, pl.ds(0, RANKS - 1)]
+        pltpu.make_async_copy(some, some, send_sem.at[step]).wait()
+
     def exchange(step, group, tiles, meanwhile=None):
         me, place, others = group
         for j in range(RANKS):
@@ -225,6 +229,8 @@
         recv[step, pl.ds(me, 1)] = send[step, pl.ds(me, 1)]
         if meanwhile is not None:
             meanwhile()
+        if step:
+            sent(step - 1)
         some = recv.at[step, pl.ds(0, RANKS - 1)]
         pltpu.make_async_copy(some, some, recv_sem.at[step]).wait()
         return [recv[step, j] for j in range(RANKS)]
@@ -243,9 +249,7 @@
                 out_ref[pl.ds(c * 32 + 2 * t + z, 8, stride=4), :] = result[
                     start : start + 8, 128 * t : 128 * t + 128
                 ]
-    for step in range(4):
-        some = send.at[step, pl.ds(0, RANKS - 1)]
-        pltpu.make_async_copy(some, some, send_sem.at[step]).wait()
+    sent(3)
 
 
 def step_kernel(
@@ -516,12 +520,12 @@
 
         lax.fori_loop(0, 8, turn, 0)
         hid_in[...] = hid_f[...].astype(BF16)
+        for copy in copies.values():
+            copy.wait_send()
 
     for load in loads[6:]:
         load.wait()
     project(u_ref, tables, vel_next, send, recv, tile_send_sem, tile_recv_sem, store_states)
-    for copy in copies.values():
-        copy.wait_send()
 
 
 def hand_on_kernel(*refs):

time: 45.2 us -> 45.2 us (level)
  no operation moved by 1% of the time
where the time goes in v10:
time: 45.2 us; the launch traced here: 45.1 us
  Pallas kernels  44.4 us (98%)
  between operations  0.64 us (1%)
    pallas_call x1, Pallas kernels, per_device(): pl.pallas_call(step_kernel, out_shape=tuple((pltpu.VMEM(r.shape, r.dtype)...  43.5 us
    pallas_call x1, Pallas kernels, per_device(): pl.pallas_call(hand_on_kernel, out_shape=results, in_specs=[vmem] * 3, ou...  0.91 us

profile of v10, /device:TPU:1, one launch (start us, length us, event | category | flops | bytes accessed | tf_op | source)
XLA Modules:
  0.0 45.1 jit_solution(8543688643429403611)
XLA Ops:
  0.6 43.5 %shard_map.139 = (bf16[1024,128]{1,0:T(8,128)(2,1)S(1)}, f32[1024,128]{1,0:T(8,128)S(1)}, f32[96,128]{1,0:T(8,128)S(1)}) custom-call(f32[96,128]{1,0:T(8,128)} %bitcast.35, bf16[1024,128]{1,0:T(8,128)(2,1)} %bitcast.33, f32[1024,128]{1,0:T(8,128)} %bitcast.32, bf16[945,128]{1,0:T(8,128)(2,1)} %bitcast.34, f32[1,128]{1,0:T(1,128)} %bitcast.36, ...), custom_call_target="tpu_custom_call" | custom-call | tf_op jit(solution)/shard_map/pallas_call | solution.py:559
  44.2 0.9 %shard_map.140 = (bf16[1024,128]{1,0:T(8,128)(2,1)}, f32[1024,128]{1,0:T(8,128)}, f32[96,128]{1,0:T(8,128)}) custom-call(bf16[1024,128]{1,0:T(8,128)(2,1)S(1)} %get-tuple-element.9.refs_0_, f32[1024,128]{1,0:T(8,128)S(1)} %get-tuple-element.10.refs_1_, f32[96,128]{1,0:T(8,128)S(1)} %get-tuple-element.11.refs_2_), custom_call_target="tpu_custom_call" | custom-call | tf_op jit(solution)/shard_map/pallas_call | solution.py:609
